TPU v7x, 256 devices: a whole 4x4x8 slice. The times are simulated.
256 devices in a mesh: blk: 32 (over y_hi, z, core), head: 8 (over x, y_lo).
Axes of the slice: x: 4, y: 4 (y_hi: 2, y_lo: 2; y = y_hi * 2 + y_lo), z: 8, core: 2. Of those that a mesh axis runs over, the one named last changes fastest.
Arguments:
- query_content: bfloat16 [32, 128, 64, 128], P('blk', None, 'head'), may hold values from -12 to 12
- query_rotary: bfloat16 [32, 64, 64, 128], P('blk', 'head'), may hold values from -48 to 48
- prompt_latent: bfloat16 [512, 4096], P(None, 'blk'), may hold values from -7 to 7
- prompt_rotary: bfloat16 [64, 4096], P(None, 'blk'), may hold values from -6 to 6
- reply_latent: bfloat16 [32, 512, 128], P('blk'), may hold values from -6 to 6
- reply_rotary: bfloat16 [32, 64, 128], P('blk'), may hold values from -6 to 6
- key_weight: bfloat16 [64, 128, 512], P('head'), may hold values from -0.25 to 0.25
- value_weight: bfloat16 [64, 512, 128], P('head'), may hold values from -1 to 1
- output_weight: bfloat16 [64, 128, 3584], P('head'), may hold values from -0.125 to 0.125
- lengths: int32 [32], P('blk'), may hold values from 32 to 128, as said below
- offsets: int32 [32], P('blk'), may hold values from 1024 to 4096, as said below
Outputs:
- layer_output: bfloat16 [128, 32, 3584], P('head', 'blk')
Inputs may be any that keep to these rules, and one draw needn't show every extreme that they name: `lengths`: some reply has all 128 slots. `offsets`: some reply sees all 4096 positions.
All inputs are finite; a program needn't handle non-finite values.
Results may differ from a plain program's by a relative error of at most 0.02.
Values may be sent and summed in bfloat16 or wider, within the bound.
No kernel may reach another device: no remote copies, remote signals or barrier semaphores. Data moves between devices by JAX's collectives and lax.ppermute only.
A program may use at most 64 MiB of HBM per device.

v0:
```python
import math

import jax
import jax.numpy as jnp
from jax import lax
from jax.sharding import PartitionSpec as P

NEGATIVE = -1e30


def body(
    query_content,
    query_rotary,
    prompt_latent,
    prompt_rotary,
    reply_latent,
    reply_rotary,
    key_weight,
    value_weight,
    output_weight,
    lengths,
    offsets,
):
    scale = (query_content.shape[-1] + query_rotary.shape[2]) ** (-0.5)
    reply_rows = query_content.shape[1]
    query_latent = jnp.einsum(
        "rthn,hnc->rhtc", query_content, key_weight, preferred_element_type=jnp.float32
    ).astype(jnp.bfloat16)

    def take_keys(state, latent, rotary, places):
        peak, total, summed = state
        scores = scale * (
            jnp.einsum("rhtc,cn->rhtn", query_latent, latent, preferred_element_type=jnp.float32)
            + jnp.einsum("rhet,en->rhtn", query_rotary, rotary, preferred_element_type=jnp.float32)
        )
        visible = places[None, :] < offsets[:, None]
        scores = jnp.where(visible[:, None, None, :], scores, NEGATIVE)
        new_peak = jnp.maximum(peak, jnp.max(scores, axis=-1))
        factor = jnp.exp(peak - new_peak)
        weights = jnp.exp(scores - new_peak[..., None])
        total = total * factor + jnp.sum(weights, axis=-1)
        summed = summed * factor[..., None] + jnp.einsum(
            "rhtn,cn->rhtc",
            weights.astype(jnp.bfloat16),
            latent,
            preferred_element_type=jnp.float32,
        )
        return (new_peak, total, summed)

    own_scores = scale * (
        jnp.einsum("rhtc,rcn->rhtn", query_latent, reply_latent, preferred_element_type=jnp.float32)
        + jnp.einsum(
            "rhet,ren->rhtn", query_rotary, reply_rotary, preferred_element_type=jnp.float32
        )
    )
    positions = jnp.arange(reply_rows, dtype=jnp.int32)
    causal = positions[:, None] >= positions[None, :]
    own_scores = jnp.where(causal[None, None], own_scores, NEGATIVE)
    own_peak = jnp.max(own_scores, axis=-1)
    own_weights = jnp.exp(own_scores - own_peak[..., None])
    starting = (
        own_peak,
        jnp.sum(own_weights, axis=-1),
        jnp.einsum(
            "rhtn,rcn->rhtc",
            own_weights.astype(jnp.bfloat16),
            reply_latent,
            preferred_element_type=jnp.float32,
        ),
    )
    piece = (
        lax.all_gather(prompt_latent, "blk", axis=1, tiled=True),
        lax.all_gather(prompt_rotary, "blk", axis=1, tiled=True),
    )
    count = piece[0].shape[1]
    places = jnp.arange(count, dtype=jnp.int32)
    latent = piece[0]
    rotary = piece[1]
    count = latent.shape[1]
    width = math.gcd(count, 512)

    def advance(index, inner):
        begin = index * width
        return take_keys(
            inner,
            lax.dynamic_slice_in_dim(latent, begin, width, 1),
            lax.dynamic_slice_in_dim(rotary, begin, width, 1),
            lax.dynamic_slice_in_dim(places, begin, width, 0),
        )

    final = lax.fori_loop(0, count // width, advance, starting)
    peak, total, summed = final
    latent_out = (summed / total[..., None]).astype(jnp.bfloat16)
    values = jnp.einsum(
        "rhtc,hcv->trhv", latent_out, value_weight, preferred_element_type=jnp.float32
    ).astype(jnp.bfloat16)
    term = jnp.einsum("trhv,hvd->trd", values, output_weight, preferred_element_type=jnp.float32)
    row_index = jnp.arange(
        reply_rows // lax.axis_size("head") * lax.axis_size("head"), dtype=jnp.int32
    )
    live = row_index[:, None] < lengths[None, :]
    return lax.psum_scatter(
        jnp.where(live[:, :, None], term, 0.0).astype(jnp.bfloat16),
        "head",
        scatter_dimension=0,
        tiled=True,
    )


def solution(mesh):
    placed = (
        P("blk", None, "head", None),
        P("blk", "head", None, None),
        P(None, "blk"),
        P(None, "blk"),
        P("blk", None, None),
        P("blk", None, None),
        P("head", None, None),
        P("head", None, None),
        P("head", None, None),
        P("blk"),
        P("blk"),
    )
    return jax.shard_map(
        body, mesh=mesh, in_specs=placed, out_specs=P("head", "blk", None), check_vma=False
    )
```

profile of v0, /device:TPU:48, one launch (start us, length us, event | category | flops | bytes accessed | tf_op | source)
XLA Modules:
  0.0 202.4 jit_solution(10374669301979798219)
XLA Ops:
  6.5 1.8 copy.19
  8.3 0.0 all-gather.2.cloned.1.call-update
  8.3 0.0 reduce-scatter.2.cloned.1.call-start
  8.4 0.0 copy-start.2
  8.4 0.0 copy-start.5
  8.4 0.0 copy-start.3
  8.4 1.5 convolution_convert_fusion
  9.9 1.3 copy.20
  12.0 0.3 fusion.34
  12.2 0.4 fusion.37
  12.6 0.0 copy-start.4
  12.6 0.1 fusion.28
  12.7 0.5 convolution_bitcast_fusion.1
  13.2 0.1 copy-done.4
  13.3 41.7 %all_gather.7 = bf16[64,4096]{1,0:T(8,128)(2,1)} all-gather(bf16[64,128]{1,0:T(8,128)(2,1)S(1)} %copy-done.4), channel_id=1, replica_groups=mesh['blk'=32,'head'=8] {'blk'}, dimensions={1}, use_global_device_ids=true | all-gather | bytes 540672 | tf_op jit(solution)/shard_map/all_gather | solution.py:73
  55.1 41.3 %all-gather.2.cloned.1.call-done = bf16[512,4096]{0,1:T(8,128)(2,1)} async-done(((bf16[512,128]{0,1:T(8,128)(2,1)}), bf16[512,4096]{0,1:T(8,128)(2,1)}) %all-gather.2.cloned.1.call-update) | async-done | bytes 4194320 | tf_op jit(solution)/shard_map/all_gather | solution.py:72
  96.4 52.4 %while.17 = (s32[]{:T(128)}, f32[1,8,128]{2,1,0:T(8,128)S(1)}, f32[1,8,128]{2,1,0:T(8,128)S(1)}, f32[1,8,128,512]{3,2,1,0:T(8,128)S(1)}, s32[4096]{0:T(1024)S(1)...) while((s32[]{:T(128)}, f32[1,8,128]{2,1,0:T(8,128)S(1)}, ...), condition=%wide.region_5.6_spmd, body=%wide.region_2.5_spmd.sunk | while | flops 1146097152 | bytes 21236964 | solution.py:91
  96.4 1.4 fusion.52
  97.8 0.7 dynamic-slice_compare_fusion.2
  98.5 1.9 bitcast_reduce_fusion.2
  100.4 2.2 %bitcast_add_fusion.5 = f32[1,8,128,512]{3,2,1,0:T(8,128)S(1)} fusion(f32[1,8,128,512]{3,2,1,0:T(8,128)S(1)} %get-tuple-element.299, f32[512,8,128]{2,0,1:T(8,128)S(1)} %get-tuple-element.280, f32[8,128]{1,0:T(8,128)S(1)} %get-tuple-element.281, f32[8,128]{1,0:T(8,128)S(1)} %bitcast.128, bf16[512,4096]{0,1:T(8,128)(2,1)} %get-tuple-element.316, ...), kind=kOutput, calls=%fused_computation.clone.1 | convolution fusion | flops 538968064 | bytes 6823940 | tf_op jit(solution)/shard_map/while/body/eval_jaxpr/rhtn,cn->rhtc/dot_general | solution.py:42
  102.6 0.3 fusion.54
  103.0 1.4 fusion.52
  104.3 0.7 dynamic-slice_compare_fusion.2
  105.1 0.0 copy-done.1
  105.1 1.9 bitcast_reduce_fusion.2
  107.0 2.2 %bitcast_add_fusion.5 = f32[1,8,128,512]{3,2,1,0:T(8,128)S(1)} fusion(f32[1,8,128,512]{3,2,1,0:T(8,128)S(1)} %get-tuple-element.299, f32[512,8,128]{2,0,1:T(8,128)S(1)} %get-tuple-element.280, f32[8,128]{1,0:T(8,128)S(1)} %get-tuple-element.281, f32[8,128]{1,0:T(8,128)S(1)} %bitcast.128, bf16[512,4096]{0,1:T(8,128)(2,1)} %get-tuple-element.316, ...), kind=kOutput, calls=%fused_computation.clone.1 | convolution fusion | flops 538968064 | bytes 6823940 | tf_op jit(solution)/shard_map/while/body/eval_jaxpr/rhtn,cn->rhtc/dot_general | solution.py:42
  109.2 0.3 fusion.54
  109.5 1.4 fusion.52
  110.9 0.7 dynamic-slice_compare_fusion.2
  111.6 0.0 copy-done.1
  111.6 1.9 bitcast_reduce_fusion.2
  113.5 2.2 %bitcast_add_fusion.5 = f32[1,8,128,512]{3,2,1,0:T(8,128)S(1)} fusion(f32[1,8,128,512]{3,2,1,0:T(8,128)S(1)} %get-tuple-element.299, f32[512,8,128]{2,0,1:T(8,128)S(1)} %get-tuple-element.280, f32[8,128]{1,0:T(8,128)S(1)} %get-tuple-element.281, f32[8,128]{1,0:T(8,128)S(1)} %bitcast.128, bf16[512,4096]{0,1:T(8,128)(2,1)} %get-tuple-element.316, ...), kind=kOutput, calls=%fused_computation.clone.1 | convolution fusion | flops 538968064 | bytes 6823940 | tf_op jit(solution)/shard_map/while/body/eval_jaxpr/rhtn,cn->rhtc/dot_general | solution.py:42
  115.7 0.3 fusion.54
  116.1 1.4 fusion.52
  117.4 0.7 dynamic-slice_compare_fusion.2
  118.2 0.0 copy-done.1
  118.2 1.9 bitcast_reduce_fusion.2
  120.1 2.2 %bitcast_add_fusion.5 = f32[1,8,128,512]{3,2,1,0:T(8,128)S(1)} fusion(f32[1,8,128,512]{3,2,1,0:T(8,128)S(1)} %get-tuple-element.299, f32[512,8,128]{2,0,1:T(8,128)S(1)} %get-tuple-element.280, f32[8,128]{1,0:T(8,128)S(1)} %get-tuple-element.281, f32[8,128]{1,0:T(8,128)S(1)} %bitcast.128, bf16[512,4096]{0,1:T(8,128)(2,1)} %get-tuple-element.316, ...), kind=kOutput, calls=%fused_computation.clone.1 | convolution fusion | flops 538968064 | bytes 6823940 | tf_op jit(solution)/shard_map/while/body/eval_jaxpr/rhtn,cn->rhtc/dot_general | solution.py:42
  122.3 0.3 fusion.54
  122.6 1.4 fusion.52
  124.0 0.7 dynamic-slice_compare_fusion.2
  124.7 0.0 copy-done.1
  124.7 1.9 bitcast_reduce_fusion.2
  126.6 2.2 %bitcast_add_fusion.5 = f32[1,8,128,512]{3,2,1,0:T(8,128)S(1)} fusion(f32[1,8,128,512]{3,2,1,0:T(8,128)S(1)} %get-tuple-element.299, f32[512,8,128]{2,0,1:T(8,128)S(1)} %get-tuple-element.280, f32[8,128]{1,0:T(8,128)S(1)} %get-tuple-element.281, f32[8,128]{1,0:T(8,128)S(1)} %bitcast.128, bf16[512,4096]{0,1:T(8,128)(2,1)} %get-tuple-element.316, ...), kind=kOutput, calls=%fused_computation.clone.1 | convolution fusion | flops 538968064 | bytes 6823940 | tf_op jit(solution)/shard_map/while/body/eval_jaxpr/rhtn,cn->rhtc/dot_general | solution.py:42
  128.8 0.3 fusion.54
  129.2 1.4 fusion.52
  130.5 0.7 dynamic-slice_compare_fusion.2
  131.3 1.9 bitcast_reduce_fusion.2
  133.2 2.2 %bitcast_add_fusion.5 = f32[1,8,128,512]{3,2,1,0:T(8,128)S(1)} fusion(f32[1,8,128,512]{3,2,1,0:T(8,128)S(1)} %get-tuple-element.299, f32[512,8,128]{2,0,1:T(8,128)S(1)} %get-tuple-element.280, f32[8,128]{1,0:T(8,128)S(1)} %get-tuple-element.281, f32[8,128]{1,0:T(8,128)S(1)} %bitcast.128, bf16[512,4096]{0,1:T(8,128)(2,1)} %get-tuple-element.316, ...), kind=kOutput, calls=%fused_computation.clone.1 | convolution fusion | flops 538968064 | bytes 6823940 | tf_op jit(solution)/shard_map/while/body/eval_jaxpr/rhtn,cn->rhtc/dot_general | solution.py:42
  135.4 0.3 fusion.54
  135.7 1.4 fusion.52
  137.1 0.7 dynamic-slice_compare_fusion.2
  137.8 1.9 bitcast_reduce_fusion.2
  139.7 2.2 %bitcast_add_fusion.5 = f32[1,8,128,512]{3,2,1,0:T(8,128)S(1)} fusion(f32[1,8,128,512]{3,2,1,0:T(8,128)S(1)} %get-tuple-element.299, f32[512,8,128]{2,0,1:T(8,128)S(1)} %get-tuple-element.280, f32[8,128]{1,0:T(8,128)S(1)} %get-tuple-element.281, f32[8,128]{1,0:T(8,128)S(1)} %bitcast.128, bf16[512,4096]{0,1:T(8,128)(2,1)} %get-tuple-element.316, ...), kind=kOutput, calls=%fused_computation.clone.1 | convolution fusion | flops 538968064 | bytes 6823940 | tf_op jit(solution)/shard_map/while/body/eval_jaxpr/rhtn,cn->rhtc/dot_general | solution.py:42
  141.9 0.3 fusion.54
  142.3 1.4 fusion.52
  143.7 0.7 dynamic-slice_compare_fusion.2
  144.4 1.9 bitcast_reduce_fusion.2
  146.3 2.2 %bitcast_add_fusion.5 = f32[1,8,128,512]{3,2,1,0:T(8,128)S(1)} fusion(f32[1,8,128,512]{3,2,1,0:T(8,128)S(1)} %get-tuple-element.299, f32[512,8,128]{2,0,1:T(8,128)S(1)} %get-tuple-element.280, f32[8,128]{1,0:T(8,128)S(1)} %get-tuple-element.281, f32[8,128]{1,0:T(8,128)S(1)} %bitcast.128, bf16[512,4096]{0,1:T(8,128)(2,1)} %get-tuple-element.316, ...), kind=kOutput, calls=%fused_computation.clone.1 | convolution fusion | flops 538968064 | bytes 6823940 | tf_op jit(solution)/shard_map/while/body/eval_jaxpr/rhtn,cn->rhtc/dot_general | solution.py:42
  148.5 0.3 fusion.54
  148.8 5.8 %fusion.20 = bf16[128,1,3584]{2,0,1:T(8,128)(2,1)} fusion(bf16[8,128,3584]{2,1,0:T(8,128)(2,1)} %param.21, bf16[8,512,128]{2,1,0:T(8,128)(2,1)} %param.20, f32[1,8,128,512]{3,2,1,0:T(8,128)S(1)} %get-tuple-element.175, f32[8,128]{1,0:T(8,128)S(1)} %bitcast.133, pred[128]{0:T(512)(128)(4,1)S(1)} %iota_compare_fusion.1), kind=kOutput, calls=%fused_computation.28 | convolution fusion | flops 1075838976 | bytes 11407488 | tf_op jit(solution)/shard_map/trhv,hvd->trd/dot_general | solution.py:97
  154.6 0.0 reduce-scatter.2.cloned.1.call-update
  154.6 40.9 %reduce-scatter.2.cloned.1.call-done = bf16[16,1,3584]{2,0,1:T(8,128)(2,1)} async-done(((bf16[128,1,3584]{2,0,1:T(8,128)(2,1)}), bf16[16,1,3584]{2,0,1:T(8,128)(2,1)}) %reduce-scatter.2.cloned.1.call-update) | async-done | bytes 114704 | tf_op jit(solution)/shard_map/reduce_scatter | solution.py:102
  (45 shorter events, 0.2 us)
Async XLA Ops:
  6.5 1.8 copy-start
  6.5 89.9 %all-gather.2.cloned.1.call-start = ((), (), s32[]{:S(2)}) async-start(), calls=%async_computation.1 | async-start | bytes 4325376 | tf_op jit(solution)/shard_map/all_gather | solution.py:72
  8.3 187.2 %reduce-scatter.2.cloned.1.call-start = ((), (), s32[]{:S(2)}) async-start(), calls=%async_computation.2 | async-start | bytes 1032192 | tf_op jit(solution)/shard_map/reduce_scatter | solution.py:102
  8.4 3.6 %copy-start.2 = (bf16[1,8,64,128]{3,2,1,0:T(8,128)(2,1)S(1)}, bf16[1,8,64,128]{3,2,1,0:T(8,128)(2,1)}, u32[]{:S(2)}) copy-start(bf16[1,8,64,128]{3,2,1,0:T(8,128)(2,1)} %param.14) | copy-start | bytes 393220
  8.4 3.6 %copy-start.5 = (bf16[1,64,128]{2,1,0:T(8,128)(2,1)S(1)}, bf16[1,64,128]{2,1,0:T(8,128)(2,1)}, u32[]{:S(2)}) copy-start(bf16[1,64,128]{2,1,0:T(8,128)(2,1)} %param.18) | copy-start | bytes 49156
  8.4 3.8 %copy-start.3 = (bf16[1,512,128]{2,1,0:T(8,128)(2,1)S(1)}, bf16[1,512,128]{2,1,0:T(8,128)(2,1)}, u32[]{:S(2)}) copy-start(bf16[1,512,128]{2,1,0:T(8,128)(2,1)} %param.17) | copy-start | bytes 393220
  12.6 0.7 copy-start.4
  96.4 2.1 %copy-start.1 = (bf16[1,8,128,512]{3,2,1,0:T(8,128)(2,1)S(1)}, bf16[1,8,128,512]{3,2,1,0:T(8,128)(2,1)}, u32[]{:S(2)}) copy-start(bf16[1,8,128,512]{3,2,1,0:T(8,128)(2,1)} %get-tuple-element.317) | copy-start | bytes 3145732 | tf_op jit(solution)/shard_map/while
  103.0 2.1 %copy-start.1 = (bf16[1,8,128,512]{3,2,1,0:T(8,128)(2,1)S(1)}, bf16[1,8,128,512]{3,2,1,0:T(8,128)(2,1)}, u32[]{:S(2)}) copy-start(bf16[1,8,128,512]{3,2,1,0:T(8,128)(2,1)} %get-tuple-element.317) | copy-start | bytes 3145732 | tf_op jit(solution)/shard_map/while
  109.5 2.1 %copy-start.1 = (bf16[1,8,128,512]{3,2,1,0:T(8,128)(2,1)S(1)}, bf16[1,8,128,512]{3,2,1,0:T(8,128)(2,1)}, u32[]{:S(2)}) copy-start(bf16[1,8,128,512]{3,2,1,0:T(8,128)(2,1)} %get-tuple-element.317) | copy-start | bytes 3145732 | tf_op jit(solution)/shard_map/while
  116.0 2.1 %copy-start.1 = (bf16[1,8,128,512]{3,2,1,0:T(8,128)(2,1)S(1)}, bf16[1,8,128,512]{3,2,1,0:T(8,128)(2,1)}, u32[]{:S(2)}) copy-start(bf16[1,8,128,512]{3,2,1,0:T(8,128)(2,1)} %get-tuple-element.317) | copy-start | bytes 3145732 | tf_op jit(solution)/shard_map/while
  122.6 2.1 %copy-start.1 = (bf16[1,8,128,512]{3,2,1,0:T(8,128)(2,1)S(1)}, bf16[1,8,128,512]{3,2,1,0:T(8,128)(2,1)}, u32[]{:S(2)}) copy-start(bf16[1,8,128,512]{3,2,1,0:T(8,128)(2,1)} %get-tuple-element.317) | copy-start | bytes 3145732 | tf_op jit(solution)/shard_map/while
  129.2 2.1 %copy-start.1 = (bf16[1,8,128,512]{3,2,1,0:T(8,128)(2,1)S(1)}, bf16[1,8,128,512]{3,2,1,0:T(8,128)(2,1)}, u32[]{:S(2)}) copy-start(bf16[1,8,128,512]{3,2,1,0:T(8,128)(2,1)} %get-tuple-element.317) | copy-start | bytes 3145732 | tf_op jit(solution)/shard_map/while
  135.7 2.1 %copy-start.1 = (bf16[1,8,128,512]{3,2,1,0:T(8,128)(2,1)S(1)}, bf16[1,8,128,512]{3,2,1,0:T(8,128)(2,1)}, u32[]{:S(2)}) copy-start(bf16[1,8,128,512]{3,2,1,0:T(8,128)(2,1)} %get-tuple-element.317) | copy-start | bytes 3145732 | tf_op jit(solution)/shard_map/while
  142.3 2.1 %copy-start.1 = (bf16[1,8,128,512]{3,2,1,0:T(8,128)(2,1)S(1)}, bf16[1,8,128,512]{3,2,1,0:T(8,128)(2,1)}, u32[]{:S(2)}) copy-start(bf16[1,8,128,512]{3,2,1,0:T(8,128)(2,1)} %get-tuple-element.317) | copy-start | bytes 3145732 | tf_op jit(solution)/shard_map/while
Sparse Core Ops, SparseCore 0:
  10.1 86.2 all-gather.1
  154.8 40.7 reduce-scatter.1
where the time goes:
time: 204 us; the launch traced here: 202 us
  waiting for transfers between devices  82.3 us (40%)
  matrix products  51.9 us (25%)
  blocking collectives  41.7 us (20%)
  between operations  14.2 us (7%)
  other arithmetic  8.39 us (4%)
  local copies, waits for them, and re-layouts  3.29 us (2%)
    all_gather x1, blocking collectives, body(): lax.all_gather(prompt_rotary, 'blk', axis=1, tiled=True)  41.7 us
    all_gather x1, waiting for transfers between devices, body(): lax.all_gather(prompt_latent, 'blk', axis=1, tiled=True)  41.3 us
    reduce_scatter x1, waiting for transfers between devices, body(): lax.psum_scatter(jnp.where(live[:, :, None], term, 0.0).astype(jnp.bfloat...  40.9 us
    dot_general x8, matrix products, take_keys(): jnp.einsum('rhtn,cn->rhtc', weights.astype(jnp.bfloat16), latent, preferr...  17.5 us
    dot_general x8, matrix products, take_keys(): jnp.einsum('rhtc,cn->rhtn', query_latent, latent, preferred_element_type=...  14.9 us
    dot_general x8, matrix products, take_keys(): jnp.einsum('rhet,en->rhtn', query_rotary, rotary, preferred_element_type=...  11.1 us
    dot_general x1, matrix products, body(): jnp.einsum('trhv,hvd->trd', values, output_weight, preferred_element_type...  5.82 us
    lt x8, other arithmetic, take_keys(): visible = places[None, :] < offsets[:, None]  5.82 us
  transfers between devices with their start and end apart: 2, of which 2 were waited for; matrix products, arithmetic and copies ran while one was open for 2% of the time, Pallas kernels for 0%

commit v1 on v0

v1 whole, which is shorter than its diff:
```python
import functools
import itertools
import math

import jax
import jax.numpy as jnp
import numpy as np
from jax import lax
from jax.experimental import pallas as pl
from jax.experimental.pallas import tpu as pltpu
from jax.sharding import PartitionSpec as P

NEGATIVE = -1e30
EMPTY = -1e29
AXES = ("blk", "head")
SIZES = (2, 8, 2, 4, 2)
KEYS = 128
DEPTH = 576
PADDED = 640


def linear(place):
    index = 0
    for value, size in zip(place, SIZES):
        index = index * size + value % size
    return index


PLACES = list(itertools.product(*map(range, SIZES)))


def pairs_from(source):
    return [(linear(source(*place)), linear(place)) for place in PLACES]


def side(core):
    return 1 - 2 * core


def fetch(far):
    def source(yh, z, core, x, yl):
        wide = (x + 2 * yl) % 4 // 2
        distance = ((1, 3), (2, 4 if core == 0 else 0))[wide][far]
        z = z - distance * side(core)
        if x % 2:
            return 1 - yh, z, core, x, 1 - yl
        return yh, z, core, x, yl

    return source


def other_core(yh, z, core, x, yl):
    return yh, z, 1 - core, x, yl


def from_x(step):
    return lambda yh, z, core, x, yl: (yh, z, core, x - step, yl)


def from_y(yh, z, core, x, yl):
    return yh, z, core, x, 1 - yl


def take(held, source):
    array, numbers = held
    pairs = pairs_from(source)
    moved = np.empty_like(numbers)
    for start, end in pairs:
        moved[end] = numbers[start]
    return lax.ppermute(array, AXES, pairs), moved


def joined(*held):
    return jnp.concatenate([h[0] for h in held], 0), np.concatenate([h[1] for h in held], 1)


def attend(query, keys, numbers, offsets, own, state, value_weight, sub, subs):
    rows = query.shape[0]
    half = rows // 2
    counts = [k.shape[0] for k in keys]
    shards = sum(counts)
    total_keys = (shards + (own is not None)) * KEYS
    block = sub * subs
    scale = (128 + 64) ** -0.5 * math.log2(math.e)
    first, last = state is None, value_weight is not None

    def kernel(numbers_ref, offsets_ref, query_ref, *refs):
        refs = list(refs)
        key_refs = [refs.pop(0) for _ in keys]
        own_ref = refs.pop(0) if first else None
        stats_in, sum_in = (None, None) if first else (refs.pop(0), refs.pop(0))
        weight_ref = refs.pop(0) if last else None
        if last:
            values_out = refs.pop(0)
        else:
            stats_out, sum_out = refs.pop(0), refs.pop(0)
        table = refs.pop(0)
        step = pl.program_id(0)

        @pl.when(step == 0)
        def _():
            at = 0
            row = lax.broadcasted_iota(jnp.int32, (16, KEYS), 0)
            lane = lax.broadcasted_iota(jnp.int32, (16, KEYS), 1)
            limit = jnp.where(row == 0, offsets_ref[0], offsets_ref[1])
            for ref, count in zip(key_refs, counts):
                for i in range(count):
                    columns = slice(at * KEYS, (at + 1) * KEYS)
                    table[0:DEPTH, columns] = ref[i]
                    hidden = (row < 2) & (numbers_ref[at] * KEYS + lane >= limit)
                    table[DEPTH : DEPTH + 16, columns] = jnp.where(hidden, NEGATIVE, 0.0).astype(jnp.bfloat16)
                    at += 1
            if first:
                columns = slice(at * KEYS, (at + 1) * KEYS)
                table[0:DEPTH, columns] = own_ref[...]
                table[DEPTH : DEPTH + 16, columns] = jnp.where(row == 1, NEGATIVE, 0.0).astype(jnp.bfloat16)
            table[DEPTH + 16 : PADDED, :] = jnp.zeros((PADDED - DEPTH - 16, total_keys), jnp.bfloat16)

        def scores(i):
            found = jnp.dot(
                query_ref[i * sub : (i + 1) * sub, :], table[...], preferred_element_type=jnp.float32
            )
            if first:
                slot = lax.broadcasted_iota(jnp.int32, (sub, KEYS), 0) % KEYS
                key = lax.broadcasted_iota(jnp.int32, (sub, KEYS), 1)
                tail = jnp.where(key <= slot, found[:, shards * KEYS :], NEGATIVE)
                found = jnp.concatenate([found[:, : shards * KEYS], tail], axis=1)
            return found

        def finish(i, found):
            part = slice(i * sub, (i + 1) * sub)
            peak = jnp.max(found, axis=1, keepdims=True)
            if first:
                peak = jnp.maximum(peak, EMPTY)
            else:
                old_peak = stats_in[part, 0:1]
                peak = jnp.maximum(peak, old_peak)
                factor = jnp.exp2((old_peak - peak) * scale)
            weights = jnp.exp2(found * scale - peak * scale)
            total = jnp.sum(weights, axis=1, keepdims=True)
            summed = lax.dot_general(
                weights.astype(jnp.bfloat16),
                table[0:512, :],
                (((1,), (1,)), ((), ())),
                preferred_element_type=jnp.float32,
            )
            if not first:
                total = total + stats_in[part, 1:2] * factor
                summed = summed + sum_in[part, :] * factor
            if not last:
                lane = lax.broadcasted_iota(jnp.int32, (sub, KEYS), 1)
                stats_out[part, :] = jnp.where(lane == 0, peak, total)
                sum_out[part, :] = summed
                return
            seen = total > 0.0
            latent = (summed / jnp.where(seen, total, 1.0)).astype(jnp.bfloat16)
            level = jnp.where(seen, peak * scale + jnp.log2(jnp.where(seen, total, 1.0)), NEGATIVE)
            high = level.astype(jnp.bfloat16).astype(jnp.float32)
            middle = (level - high).astype(jnp.bfloat16).astype(jnp.float32)
            low = level - high - middle
            lane = lax.broadcasted_iota(jnp.int32, (sub, KEYS), 1)
            parts = jnp.where(lane == 0, high, jnp.where(lane == 1, middle, low))
            values_out[part, KEYS:] = parts.astype(jnp.bfloat16)
            for j in range(sub // KEYS):
                head = lax.rem(step * (block // KEYS) + i * (sub // KEYS) + j, half // KEYS)
                values_out[i * sub + j * KEYS : i * sub + (j + 1) * KEYS, :KEYS] = jnp.dot(
                    latent[j * KEYS : (j + 1) * KEYS, :],
                    weight_ref[head],
                    preferred_element_type=jnp.float32,
                ).astype(jnp.bfloat16)

        found = scores(0)
        for i in range(subs):
            following = scores(i + 1) if i + 1 < subs else None
            finish(i, found)
            found = following

    def tall(width):
        return pl.BlockSpec((block, width), lambda i, *_: (i, 0))

    def whole(array):
        return pl.BlockSpec(array.shape, lambda i, *_: (0,) * array.ndim)

    operands, specs = [query, *keys], [tall(PADDED), *map(whole, keys)]
    if first:
        operands.append(own)
        specs.append(whole(own))
    else:
        operands += state
        specs += [tall(KEYS), tall(512)]
    if last:
        operands.append(value_weight)
        specs.append(whole(value_weight))
        shapes = [jax.ShapeDtypeStruct((rows, 2 * KEYS), jnp.bfloat16)]
        outs = [tall(2 * KEYS)]
    else:
        shapes = [jax.ShapeDtypeStruct((rows, KEYS), jnp.float32), jax.ShapeDtypeStruct((rows, 512), jnp.float32)]
        outs = [tall(KEYS), tall(512)]
    return pl.pallas_call(
        kernel,
        grid_spec=pltpu.PrefetchScalarGridSpec(
            num_scalar_prefetch=2,
            grid=(rows // block,),
            in_specs=specs,
            out_specs=outs,
            scratch_shapes=[pltpu.VMEM((PADDED, total_keys), jnp.bfloat16)],
        ),
        out_shape=shapes,
        compiler_params=pltpu.CompilerParams(vmem_limit_bytes=48 * 2**20),
        cost_estimate=pl.CostEstimate(
            flops=2 * rows * total_keys * (PADDED + 512), bytes_accessed=8 << 20, transcendentals=rows * total_keys
        ),
    )(numbers, offsets, *operands)


def project(mine, theirs, output_weight, length):
    rows = mine.shape[0]
    heads = rows // KEYS
    width = output_weight.shape[-1]
    tile = 512

    def kernel(length_ref, mine_ref, theirs_ref, weight_ref, out_ref, values):
        @pl.when(pl.program_id(0) == 0)
        def _():
            def level(ref, part):
                found = ref[part, KEYS:].astype(jnp.float32)
                return found[:, 0:1] + (found[:, 1:2] + found[:, 2:3])

            for head in range(heads):
                part = slice(head * KEYS, (head + 1) * KEYS)
                a, b = level(mine_ref, part), level(theirs_ref, part)
                top = jnp.maximum(a, b)
                a, b = jnp.exp2(a - top), jnp.exp2(b - top)
                both = mine_ref[part, :KEYS].astype(jnp.float32) * a + theirs_ref[part, :KEYS].astype(jnp.float32) * b
                slot = lax.broadcasted_iota(jnp.int32, (KEYS, KEYS), 0)
                both = jnp.where(slot < length_ref[0], both / (a + b), 0.0)
                values[:, part] = both.astype(jnp.bfloat16)

        out_ref[...] = jnp.dot(values[...], weight_ref[...], preferred_element_type=jnp.float32).astype(jnp.bfloat16)

    return pl.pallas_call(
        kernel,
        grid_spec=pltpu.PrefetchScalarGridSpec(
            num_scalar_prefetch=1,
            grid=(width // tile,),
            in_specs=[
                pl.BlockSpec(mine.shape, lambda i, *_: (0, 0)),
                pl.BlockSpec(theirs.shape, lambda i, *_: (0, 0)),
                pl.BlockSpec((rows, tile), lambda i, *_: (0, i)),
            ],
            out_specs=pl.BlockSpec((KEYS, tile), lambda i, *_: (0, i)),
            scratch_shapes=[pltpu.VMEM((KEYS, rows), jnp.bfloat16)],
        ),
        out_shape=jax.ShapeDtypeStruct((KEYS, width), jnp.bfloat16),
        compiler_params=pltpu.CompilerParams(vmem_limit_bytes=32 * 2**20),
        cost_estimate=pl.CostEstimate(flops=2 * KEYS * rows * width, bytes_accessed=2 * rows * width, transcendentals=0),
    )(length, mine, theirs, output_weight)


def body(
    query_content,
    query_rotary,
    prompt_latent,
    prompt_rotary,
    reply_latent,
    reply_rotary,
    key_weight,
    value_weight,
    output_weight,
    lengths,
    offsets,
):
    device = lax.axis_index("blk") * lax.axis_size("head") + lax.axis_index("head")
    numbers = np.array([[linear(place) // 8] for place in PLACES], np.int32)
    mine = (jnp.concatenate([prompt_latent, prompt_rotary], 0)[None], numbers)
    chip = joined(mine, take(mine, other_core))
    near, far = take(chip, fetch(0)), take(chip, fetch(1))
    groups = [[near, far]]
    groups.append([take(h, s) for h in (near, far) for s in (from_x(1), from_x(-1), from_y)])

    heads, slots = key_weight.shape[0], query_content.shape[1]
    query_latent = jnp.einsum("thn,hnc->htc", query_content[0], key_weight, preferred_element_type=jnp.float32)
    query = jnp.concatenate([query_latent.astype(jnp.bfloat16), jnp.swapaxes(query_rotary[0], 1, 2)], -1)
    query = query.reshape(heads * slots, DEPTH)
    partner = pairs_from(other_core)
    query_theirs = lax.ppermute(query, AXES, partner)
    lane = jnp.arange(PADDED - DEPTH)
    marks = [jnp.broadcast_to((lane == i).astype(jnp.bfloat16), (heads * slots, PADDED - DEPTH)) for i in (0, 1)]
    query = jnp.concatenate(
        [jnp.concatenate([query, marks[0]], 1), jnp.concatenate([query_theirs, marks[1]], 1)], 0
    )
    limits = jnp.concatenate([offsets, lax.ppermute(offsets, AXES, partner)])
    own = jnp.concatenate([reply_latent[0], reply_rotary[0]], 0)

    state = None
    for at, group in enumerate(groups):
        table = np.concatenate([h[1] for h in group], 1)
        here = lax.dynamic_index_in_dim(jnp.asarray(table), device, 0, keepdims=False)
        weight = value_weight if at + 1 == len(groups) else None
        state = attend(query, [h[0] for h in group], here, limits, own if at == 0 else None, state, weight, 256, 2)
    (values,) = state
    rows = heads * slots
    theirs = lax.ppermute(values[rows:], AXES, partner)
    term = project(values[:rows], theirs, output_weight.reshape(rows, -1), lengths)
    parts = lax.all_to_all(term, "head", 0, 0, tiled=True)
    parts = parts.reshape(8, slots // 8, -1).astype(jnp.float32)
    return jnp.sum(parts, 0).astype(jnp.bfloat16)[:, None, :]


def solution(mesh):
    placed = (
        P("blk", None, "head", None),
        P("blk", "head", None, None),
        P(None, "blk"),
        P(None, "blk"),
        P("blk", None, None),
        P("blk", None, None),
        P("head", None, None),
        P("head", None, None),
        P("head", None, None),
        P("blk"),
        P("blk"),
    )
    return jax.shard_map(
        body, mesh=mesh, in_specs=placed, out_specs=P("head", "blk", None), check_vma=False
    )
```

time: 204 us -> 93.6 us (0.46)
  waiting for transfers between devices: 82.3 us -> 10.8 us
  matrix products: 51.9 us -> 1.36 us
  Pallas kernels: 0 us -> 26.1 us
  blocking collectives: 41.7 us -> 17.1 us
  starting transfers between devices: 0.04 us -> 22.9 us
  between operations: 14.2 us -> 1.54 us
  local copies, waits for them, and re-layouts: 3.29 us -> 9.08 us
  other arithmetic: 8.39 us -> 3.74 us
    dot_general x29 -> x1, matrix products: 51.9 us -> 1.36 us  [body(): jnp.einsum('thn,hnc->htc', query_content[0], key_weight, preferred_elemen...]
    all_gather x1 -> x0, blocking collectives: 41.7 us -> none  [body(): lax.all_gather(prompt_rotary, 'blk', axis=1, tiled=True)]
    all_gather x1 -> x0, waiting for transfers between devices: 41.3 us -> none  [body(): lax.all_gather(prompt_latent, 'blk', axis=1, tiled=True)]
    reduce_scatter x1 -> x0, waiting for transfers between devices: 40.9 us -> none  [body(): lax.psum_scatter(jnp.where(live[:, :, None], term, 0.0).astype(jnp.bfloat...]
    pallas_call x0 -> x3, Pallas kernels: none -> 26.1 us  [the longest x2 21.1 us: attend(): pl.pallas_call(kernel, grid_spec=pltpu.PrefetchScalarGridSpec(num_scalar_...]
    ppermute x0 -> x12, starting transfers between devices: none -> 22.9 us  [the longest x9 22.7 us: take(): return (lax.ppermute(array, AXES, pairs), moved)]
    all_to_all x0 -> x1, blocking collectives: none -> 17.1 us  [body(): parts = lax.all_to_all(term, 'head', 0, 0, tiled=True)]
    ppermute x0 -> x12, waiting for transfers between devices: none -> 10.8 us  [the longest x9 9.53 us: take(): return (lax.ppermute(array, AXES, pairs), moved)]
  transfers between devices with their start and end apart: 2 -> 12, of which waited for: 2 -> 3; matrix products, arithmetic and copies ran while one was open for 2% -> 7% of each run, Pallas kernels for 0% -> 7%
where the time goes in v1:
time: 93.6 us; the launch traced here: 92.6 us
  Pallas kernels  26.1 us (28%)
  starting transfers between devices  22.9 us (24%)
  blocking collectives  17.1 us (18%)
  waiting for transfers between devices  10.8 us (12%)
  local copies, waits for them, and re-layouts  9.08 us (10%)
  other arithmetic  3.74 us (4%)
  between operations  1.54 us (2%)
  matrix products  1.36 us (1%)
    ppermute x9, starting transfers between devices, take(): return (lax.ppermute(array, AXES, pairs), moved)  22.7 us
    pallas_call x2, Pallas kernels, attend(): pl.pallas_call(kernel, grid_spec=pltpu.PrefetchScalarGridSpec(num_scalar_...  21.1 us
    all_to_all x1, blocking collectives, body(): parts = lax.all_to_all(term, 'head', 0, 0, tiled=True)  17.1 us
    ppermute x9, waiting for transfers between devices, take(): return (lax.ppermute(array, AXES, pairs), moved)  9.53 us
    pallas_call x1, Pallas kernels, project(): pl.pallas_call(kernel, grid_spec=pltpu.PrefetchScalarGridSpec(num_scalar_...  5.03 us
    unnamed x25, local copies, waits for them, and re-layouts  3.67 us
    ppermute x1, local copies, waits for them, and re-layouts, body(): query_theirs = lax.ppermute(query, AXES, partner)  2.39 us
    concatenate x1, other arithmetic, body(): jnp.concatenate([jnp.concatenate([query, marks[0]], 1), jnp.concatenate([...  2.1 us
  transfers between devices with their start and end apart: 12, of which 3 were waited for; matrix products, arithmetic and copies ran while one was open for 7% of the time, Pallas kernels for 7%

profile of v1, /device:TPU:48, one launch (start us, length us, event | category | flops | bytes accessed | tf_op | source)
XLA Modules:
  0.0 92.6 jit_solution(5149025289205627691)
XLA Ops:
  0.0 0.0 copy-start
  0.0 1.2 %copy.17 = bf16[1,8,64,128]{2,3,1,0:T(8,128)(2,1)S(1)} copy(bf16[1,8,64,128]{3,2,1,0:T(8,128)(2,1)} %param.14) | data formatting | bytes 262144 | tf_op args[1]
  1.2 0.1 copy-done
  1.3 1.4 %convolution_convert_fusion = bf16[8,128,512]{2,1,0:T(8,128)(2,1)S(1)} fusion(bf16[8,128,512]{2,1,0:T(8,128)(2,1)S(1)} %copy-done, bf16[128,8,128]{2,1,0:T(8,128)(2,1)} %bitcast.24), kind=kOutput, calls=%fused_computation.1 | convolution fusion | flops 134742016 | bytes 2359296 | tf_op jit(solution)/shard_map/thn,hnc->htc/dot_general | solution.py:282
  2.7 0.0 copy-start.6
  2.7 0.0 copy-start.8
  2.7 0.0 copy-start.7
  2.7 0.0 copy-start.9
  2.7 0.1 pad_maximum_fusion
  2.8 0.0 copy-start.5
  2.8 1.5 %copy.18 = bf16[1024,576]{0,1:T(8,128)(2,1)} copy(bf16[1024,576]{1,0:T(8,128)(2,1)S(1)} %bitcast.21) | data formatting | bytes 2359296 | tf_op jit(solution)/shard_map/reshape | solution.py:284
  4.3 0.0 collective-permute-start.1
  4.3 0.0 copy-done.6
  4.3 0.0 copy-done.8
  4.3 0.6 collective-permute-start.2
  4.9 0.1 collective-permute-start
  5.7 1.4 %collective-permute-done.2 = bf16[1,576,128]{2,1,0:T(8,128)(2,1)S(1)} collective-permute-done((bf16[1,576,128]{2,1,0:T(8,128)(2,1)S(1)}, bf16[1,576,128]{2,1,0:T(8,128)(2,1)S(1)}, u32[]{:S(2)}, u32[]{:S(2)}) %collective-permute-start.2) | collective-permute-done | bytes 147488 | tf_op jit(solution)/shard_map/ppermute | solution.py:70
  7.1 0.0 copy-done.5
  7.1 7.7 %collective-permute-start.7 = (bf16[2,576,128]{2,1,0:T(8,128)(2,1)S(1)}, bf16[2,576,128]{2,1,0:T(8,128)(2,1)S(1)}, u32[]{:S(2)}, u32[]{:S(2)}) collective-permute-start(bf16[2,576,128]{2,1,0:T(8,128)(2,1)S(1)} %pad_maximum_fusion.1), channel_id=1, source_target_pairs={{80,0},{65,1},{211,2},{194,3},{68,4},{85,5},{199,6},{214,7},{56,8}... | collective-permute-start | bytes 884744 | tf_op jit(solution)/shard_map/ppermute | solution.py:70
  14.9 0.7 dynamic-slice_bitcast_fusion.numbers_ref
  15.6 1.0 %collective-permute-start.3 = (bf16[2,576,128]{2,1,0:T(8,128)(2,1)S(1)}, bf16[2,576,128]{2,1,0:T(8,128)(2,1)S(1)}, u32[]{:S(2)}, u32[]{:S(2)}) collective-permute-start(bf16[2,576,128]{2,1,0:T(8,128)(2,1)S(1)} %pad_maximum_fusion.1), channel_id=1, source_target_pairs={{112,0},{97,1},{243,2},{226,3},{100,4},{117,5},{231,6},{246,7},{24... | collective-permute-start | bytes 884744 | tf_op jit(solution)/shard_map/ppermute | solution.py:70
  16.6 8.1 %collective-permute-done.7.refs_1_ = bf16[2,576,128]{2,1,0:T(8,128)(2,1)S(1)} collective-permute-done((bf16[2,576,128]{2,1,0:T(8,128)(2,1)S(1)}, bf16[2,576,128]{2,1,0:T(8,128)(2,1)S(1)}, u32[]{:S(2)}, u32[]{:S(2)}) %collective-permute-start.7) | collective-permute-done | bytes 294944 | tf_op jit(solution)/shard_map/ppermute | solution.py:70
  24.7 5.5 %collective-permute-start.10 = (bf16[2,576,128]{2,1,0:T(8,128)(2,1)S(1)}, bf16[2,576,128]{2,1,0:T(8,128)(2,1)S(1)}, u32[]{:S(2)}, u32[]{:S(2)}) collective-permute-start(bf16[2,576,128]{2,1,0:T(8,128)(2,1)S(1)} %collective-permute-done.7.refs_1_), channel_id=1, source_target_pairs={{1,0},{0,1},{3,2},{2,3},{5,4},{4,5},{7,6},{6,7},{9,8},{8,9},{11,10... | collective-permute-start | bytes 884744 | tf_op jit(solution)/shard_map/ppermute | solution.py:70
  30.2 0.7 dynamic-slice_bitcast_fusion.1.numbers_ref
  30.9 0.0 copy-done.7
  30.9 0.0 copy-done.9
  30.9 0.0 collective-permute-done
  30.9 0.7 pad_add_fusion.offsets_ref
  31.6 0.0 collective-permute-done.3.refs_0_
  31.6 0.9 collective-permute-start.4
  32.5 2.4 %collective-permute-start.5 = (bf16[2,576,128]{2,1,0:T(8,128)(2,1)S(1)}, bf16[2,576,128]{2,1,0:T(8,128)(2,1)}, u32[]{:S(2)}, u32[]{:S(2)}) collective-permute-start(bf16[2,576,128]{2,1,0:T(8,128)(2,1)S(1)} %collective-permute-done.3.refs_0_), channel_id=1, source_target_pairs={{2,0},{3,1},{4,2},{5,3},{6,4},{7,5},{0,6},{1,7},{10,8},{11,9},{12,... | collective-permute-start | bytes 884744 | tf_op jit(solution)/shard_map/ppermute | solution.py:70
  34.9 1.4 %collective-permute-start.6 = (bf16[2,576,128]{2,1,0:T(8,128)(2,1)S(1)}, bf16[2,576,128]{2,1,0:T(8,128)(2,1)}, u32[]{:S(2)}, u32[]{:S(2)}) collective-permute-start(bf16[2,576,128]{2,1,0:T(8,128)(2,1)S(1)} %collective-permute-done.3.refs_0_), channel_id=1, source_target_pairs={{1,0},{0,1},{3,2},{2,3},{5,4},{4,5},{7,6},{6,7},{9,8},{8,9},{11,10... | collective-permute-start | bytes 884744 | tf_op jit(solution)/shard_map/ppermute | solution.py:70
  36.3 0.0 collective-permute-done.1
  36.3 0.3 collective-permute-start.8
  36.5 2.4 %copy.19 = bf16[1024,576]{1,0:T(8,128)(2,1)} copy(bf16[1024,576]{0,1:T(8,128)(2,1)} %collective-permute-done.1) | data formatting | bytes 2359296 | tf_op jit(solution)/shard_map/ppermute | solution.py:286
  38.9 0.0 collective-permute-done.10.refs_5_
  38.9 3.0 %collective-permute-start.9 = (bf16[2,576,128]{2,1,0:T(8,128)(2,1)S(1)}, bf16[2,576,128]{2,1,0:T(8,128)(2,1)S(1)}, u32[]{:S(2)}, u32[]{:S(2)}) collective-permute-start(bf16[2,576,128]{2,1,0:T(8,128)(2,1)S(1)} %collective-permute-done.7.refs_1_), channel_id=1, source_target_pairs={{2,0},{3,1},{4,2},{5,3},{6,4},{7,5},{0,6},{1,7},{10,8},{11,9},{12,... | collective-permute-start | bytes 884744 | tf_op jit(solution)/shard_map/ppermute | solution.py:70
  42.0 2.1 %maximum_maximum_fusion.query_ref = bf16[2048,640]{1,0:T(8,128)(2,1)S(1)} fusion(bf16[1024,64]{1,0:T(8,128)(2,1)S(1)} %broadcast_in_dim.13, bf16[1024,576]{1,0:T(8,128)(2,1)} %copy.19, bf16[1024,64]{1,0:T(8,128)(2,1)S(1)} %broadcast_in_dim.12, bf16[1024,576]{1,0:T(8,128)(2,1)} %bitcast.22), kind=kLoop, calls=%fused_computation | loop fusion | flops 10485760 | bytes 5242880 | tf_op jit(solution)/shard_map/concatenate | solution.py:289
  44.1 0.0 copy-start.1
  44.1 0.0 copy-start.2
  44.1 6.7 %shard_map.127 = (f32[2048,128]{1,0:T(8,128)S(1)}, f32[2048,512]{1,0:T(8,128)}) custom-call(s32[4]{0:T(128)S(1)} %dynamic-slice_bitcast_fusion.numbers_ref, s32[2]{0:T(128)S(1)} %pad_add_fusion.offsets_ref, bf16[2048,640]{1,0:T(8,128)(2,1)S(1)} %maximum_maximum_fusion.query_ref, bf16[2,576,128]{2,1,0:T(8,128)(2,1)S(1)} %collective-permute-done.3.refs_0_, ...), custom_call_target="tpu_custom_call" | custom-call | flops 3019898880 | bytes 8388608 | tf_op jit(solution)/shard_map/pallas_call | solution.py:199
  50.8 0.0 copy-done.1
  50.8 0.0 copy-start.3
  50.8 1.0 %copy-done.3 = f32[2048,128]{1,0:T(8,128)} copy-done((f32[2048,128]{1,0:T(8,128)}, f32[2048,128]{1,0:T(8,128)S(1)}, u32[]{:S(2)}) %copy-start.3) | copy-done | bytes 1048600
  51.8 0.0 collective-permute-done.4.refs_0_
  51.8 0.0 collective-permute-done.5.refs_1_
  51.8 0.0 collective-permute-done.6.refs_2_
  51.8 0.0 collective-permute-done.8.refs_3_
  51.8 0.0 collective-permute-done.9.refs_4_
  51.8 0.0 slice-start
  51.8 0.0 copy-done.2
  51.8 0.0 copy-start.4
  51.8 1.4 %copy-done.4 = f32[2048,128]{1,0:T(8,128)S(1)} copy-done((f32[2048,128]{1,0:T(8,128)S(1)}, f32[2048,128]{1,0:T(8,128)}, u32[]{:S(2)}) %copy-start.4) | copy-done | bytes 1048600
  53.2 0.0 slice-start.1
  53.2 14.4 %shard_map.128 = bf16[2048,256]{1,0:T(8,128)(2,1)S(1)} custom-call(s32[12]{0:T(128)S(1)} %dynamic-slice_bitcast_fusion.1.numbers_ref, s32[2]{0:T(128)S(1)} %pad_add_fusion.offsets_ref, bf16[2048,640]{1,0:T(8,128)(2,1)} %copy-done.1, bf16[2,576,128]{2,1,0:T(8,128)(2,1)S(1)} %collective-permute-done.4.refs_0_, ...), custom_call_target="tpu_custom_call" | custom-call | flops 7247757312 | bytes 8388608 | tf_op jit(solution)/shard_map/pallas_call | solution.py:199
  67.6 0.1 fusion.1
  67.7 0.1 collective-permute-start.11
  68.4 1.2 %collective-permute-done.11.theirs_ref = bf16[1024,256]{1,0:T(8,128)(2,1)S(1)} collective-permute-done((bf16[1024,256]{1,0:T(8,128)(2,1)S(1)}, bf16[1024,256]{1,0:T(8,128)(2,1)S(1)}, u32[]{:S(2)}, u32[]{:S(2)}) %collective-permute-start.11) | collective-permute-done | bytes 524320 | tf_op jit(solution)/shard_map/ppermute | solution.py:303
  69.7 0.0 slice-done
  69.7 0.0 slice-done.1
  69.7 5.0 %shard_map.129 = bf16[128,3584]{1,0:T(8,128)(2,1)S(1)} custom-call(s32[1]{0:T(128)S(6)} %copy.22.length_ref, bf16[1024,256]{1,0:T(8,128)(2,1)S(1)} %get-tuple-element.10.mine_ref, bf16[1024,256]{1,0:T(8,128)(2,1)S(1)} %collective-permute-done.11.theirs_ref, bf16[1024,3584]{1,0:T(8,128)(2,1)S(1)} %bitcast.19), custom_call_target="tpu_custom_call" | custom-call | flops 939524096 | bytes 7340032 | tf_op jit(solution)/shard_map/pallas_call | solution.py:241
  74.7 17.1 %all_to_all.9 = bf16[8,16,3584]{2,1,0:T(8,128)(2,1)S(1)} all-to-all(bf16[8,16,3584]{2,1,0:T(8,128)(2,1)S(1)} %bitcast.20), channel_id=1, replica_groups=mesh['blk'=32,'head'=8] {'head'}, dimensions={0} | all-to-all | bytes 1835008 | tf_op jit(solution)/shard_map/all_to_all | solution.py:305
  91.8 0.8 reduce_sum.12
  (8 shorter events, 0.1 us)
Async XLA Ops:
  0.0 1.3 %copy-start = (bf16[8,128,512]{2,1,0:T(8,128)(2,1)S(1)}, bf16[8,128,512]{2,1,0:T(8,128)(2,1)}, u32[]{:S(2)}) copy-start(bf16[8,128,512]{2,1,0:T(8,128)(2,1)} %param.19) | copy-start | bytes 3145732
  2.7 1.7 %copy-start.6 = (bf16[512,128]{1,0:T(8,128)(2,1)S(1)}, bf16[512,128]{1,0:T(8,128)(2,1)}, u32[]{:S(2)}) copy-start(bf16[512,128]{1,0:T(8,128)(2,1)} %param.15) | copy-start | bytes 393220
  2.7 1.7 %copy-start.8 = (bf16[64,128]{1,0:T(8,128)(2,1)S(1)}, bf16[64,128]{1,0:T(8,128)(2,1)}, u32[]{:S(2)}) copy-start(bf16[64,128]{1,0:T(8,128)(2,1)} %param.16) | copy-start | bytes 49156
  2.7 28.2 %copy-start.7 = (bf16[1,512,128]{2,1,0:T(8,128)(2,1)S(1)}, bf16[1,512,128]{2,1,0:T(8,128)(2,1)}, u32[]{:S(2)}) copy-start(bf16[1,512,128]{2,1,0:T(8,128)(2,1)} %param.17) | copy-start | bytes 393220
  2.7 28.2 %copy-start.9 = (bf16[1,64,128]{2,1,0:T(8,128)(2,1)S(1)}, bf16[1,64,128]{2,1,0:T(8,128)(2,1)}, u32[]{:S(2)}) copy-start(bf16[1,64,128]{2,1,0:T(8,128)(2,1)} %param.18) | copy-start | bytes 49156
  2.8 4.3 %copy-start.5 = (bf16[8,128,576]{2,1,0:T(8,128)(2,1)}, bf16[8,128,576]{2,1,0:T(8,128)(2,1)S(1)}, u32[]{:S(2)}) copy-start(bf16[8,128,576]{2,1,0:T(8,128)(2,1)S(1)} %pad_maximum_fusion) | copy-start | bytes 3538948
  4.3 31.9 %collective-permute-start.1 = (bf16[1024,576]{0,1:T(8,128)(2,1)}, bf16[1024,576]{0,1:T(8,128)(2,1)}, u32[]{:S(2)}, u32[]{:S(2)}) collective-permute-start(bf16[1024,576]{0,1:T(8,128)(2,1)} %copy.18), channel_id=1, source_target_pairs={{8,0},{9,1},{10,2},{11,3},{12,4},{13,5},{14,6},{15,7},{0,8},{1,9},... | collective-permute-start | bytes 3538952 | tf_op jit(solution)/shard_map/ppermute | solution.py:286
  4.3 2.7 %collective-permute-start.2 = (bf16[1,576,128]{2,1,0:T(8,128)(2,1)S(1)}, bf16[1,576,128]{2,1,0:T(8,128)(2,1)S(1)}, u32[]{:S(2)}, u32[]{:S(2)}) collective-permute-start(bf16[1,576,128]{2,1,0:T(8,128)(2,1)S(1)} %maximum_bitcast_fusion), channel_id=1, source_target_pairs={{8,0},{9,1},{10,2},{11,3},{12,4},{13,5},{14,6},{15,7},{0,8},{1,9},... | collective-permute-start | bytes 442376 | tf_op jit(solution)/shard_map/ppermute | solution.py:70
  4.9 26.0 %collective-permute-start = (s32[1]{0:T(128)}, s32[1]{0:T(128)}, u32[]{:S(2)}, u32[]{:S(2)}) collective-permute-start(s32[1]{0:T(128)} %param.23), channel_id=1, source_target_pairs={{8,0},{9,1},{10,2},{11,3},{12,4},{13,5},{14,6},{15,7},{0,8},{1,9},... | collective-permute-start | bytes 20 | tf_op jit(solution)/shard_map/ppermute | solution.py:292
  7.1 17.6 %collective-permute-start.7 = (bf16[2,576,128]{2,1,0:T(8,128)(2,1)S(1)}, bf16[2,576,128]{2,1,0:T(8,128)(2,1)S(1)}, u32[]{:S(2)}, u32[]{:S(2)}) collective-permute-start(bf16[2,576,128]{2,1,0:T(8,128)(2,1)S(1)} %pad_maximum_fusion.1), channel_id=1, source_target_pairs={{80,0},{65,1},{211,2},{194,3},{68,4},{85,5},{199,6},{214,7},{56,8}... | collective-permute-start | bytes 884744 | tf_op jit(solution)/shard_map/ppermute | solution.py:70
  15.6 16.0 %collective-permute-start.3 = (bf16[2,576,128]{2,1,0:T(8,128)(2,1)S(1)}, bf16[2,576,128]{2,1,0:T(8,128)(2,1)S(1)}, u32[]{:S(2)}, u32[]{:S(2)}) collective-permute-start(bf16[2,576,128]{2,1,0:T(8,128)(2,1)S(1)} %pad_maximum_fusion.1), channel_id=1, source_target_pairs={{112,0},{97,1},{243,2},{226,3},{100,4},{117,5},{231,6},{246,7},{24... | collective-permute-start | bytes 884744 | tf_op jit(solution)/shard_map/ppermute | solution.py:70
  24.7 14.2 %collective-permute-start.10 = (bf16[2,576,128]{2,1,0:T(8,128)(2,1)S(1)}, bf16[2,576,128]{2,1,0:T(8,128)(2,1)S(1)}, u32[]{:S(2)}, u32[]{:S(2)}) collective-permute-start(bf16[2,576,128]{2,1,0:T(8,128)(2,1)S(1)} %collective-permute-done.7.refs_1_), channel_id=1, source_target_pairs={{1,0},{0,1},{3,2},{2,3},{5,4},{4,5},{7,6},{6,7},{9,8},{8,9},{11,10... | collective-permute-start | bytes 884744 | tf_op jit(solution)/shard_map/ppermute | solution.py:70
  31.6 20.1 %collective-permute-start.4 = (bf16[2,576,128]{2,1,0:T(8,128)(2,1)S(1)}, bf16[2,576,128]{2,1,0:T(8,128)(2,1)S(1)}, u32[]{:S(2)}, u32[]{:S(2)}) collective-permute-start(bf16[2,576,128]{2,1,0:T(8,128)(2,1)S(1)} %collective-permute-done.3.refs_0_), channel_id=1, source_target_pairs={{6,0},{7,1},{0,2},{1,3},{2,4},{3,5},{4,6},{5,7},{14,8},{15,9},{8,1... | collective-permute-start | bytes 884744 | tf_op jit(solution)/shard_map/ppermute | solution.py:70
  32.5 19.3 %collective-permute-start.5 = (bf16[2,576,128]{2,1,0:T(8,128)(2,1)S(1)}, bf16[2,576,128]{2,1,0:T(8,128)(2,1)}, u32[]{:S(2)}, u32[]{:S(2)}) collective-permute-start(bf16[2,576,128]{2,1,0:T(8,128)(2,1)S(1)} %collective-permute-done.3.refs_0_), channel_id=1, source_target_pairs={{2,0},{3,1},{4,2},{5,3},{6,4},{7,5},{0,6},{1,7},{10,8},{11,9},{12,... | collective-permute-start | bytes 884744 | tf_op jit(solution)/shard_map/ppermute | solution.py:70
  34.9 16.9 %collective-permute-start.6 = (bf16[2,576,128]{2,1,0:T(8,128)(2,1)S(1)}, bf16[2,576,128]{2,1,0:T(8,128)(2,1)}, u32[]{:S(2)}, u32[]{:S(2)}) collective-permute-start(bf16[2,576,128]{2,1,0:T(8,128)(2,1)S(1)} %collective-permute-done.3.refs_0_), channel_id=1, source_target_pairs={{1,0},{0,1},{3,2},{2,3},{5,4},{4,5},{7,6},{6,7},{9,8},{8,9},{11,10... | collective-permute-start | bytes 884744 | tf_op jit(solution)/shard_map/ppermute | solution.py:70
  36.3 15.5 %collective-permute-start.8 = (bf16[2,576,128]{2,1,0:T(8,128)(2,1)S(1)}, bf16[2,576,128]{2,1,0:T(8,128)(2,1)}, u32[]{:S(2)}, u32[]{:S(2)}) collective-permute-start(bf16[2,576,128]{2,1,0:T(8,128)(2,1)S(1)} %collective-permute-done.7.refs_1_), channel_id=1, source_target_pairs={{6,0},{7,1},{0,2},{1,3},{2,4},{3,5},{4,6},{5,7},{14,8},{15,9},{8,1... | collective-permute-start | bytes 884744 | tf_op jit(solution)/shard_map/ppermute | solution.py:70
  38.9 12.9 %collective-permute-start.9 = (bf16[2,576,128]{2,1,0:T(8,128)(2,1)S(1)}, bf16[2,576,128]{2,1,0:T(8,128)(2,1)S(1)}, u32[]{:S(2)}, u32[]{:S(2)}) collective-permute-start(bf16[2,576,128]{2,1,0:T(8,128)(2,1)S(1)} %collective-permute-done.7.refs_1_), channel_id=1, source_target_pairs={{2,0},{3,1},{4,2},{5,3},{6,4},{7,5},{0,6},{1,7},{10,8},{11,9},{12,... | collective-permute-start | bytes 884744 | tf_op jit(solution)/shard_map/ppermute | solution.py:70
  44.1 6.7 %copy-start.1 = (bf16[2048,640]{1,0:T(8,128)(2,1)}, bf16[2048,640]{1,0:T(8,128)(2,1)S(1)}, u32[]{:S(2)}) copy-start(bf16[2048,640]{1,0:T(8,128)(2,1)S(1)} %maximum_maximum_fusion.query_ref) | copy-start | bytes 7864324
  44.1 7.7 %copy-start.2 = (bf16[8,512,128]{2,1,0:T(8,128)(2,1)S(1)}, bf16[8,512,128]{2,1,0:T(8,128)(2,1)}, u32[]{:S(2)}) copy-start(bf16[8,512,128]{2,1,0:T(8,128)(2,1)} %refs_8_.1) | copy-start | bytes 3145732
  50.8 1.0 %copy-start.3 = (f32[2048,128]{1,0:T(8,128)}, f32[2048,128]{1,0:T(8,128)S(1)}, u32[]{:S(2)}) copy-start(f32[2048,128]{1,0:T(8,128)S(1)} %get-tuple-element.7.refs_6_) | copy-start | bytes 3145732
  51.8 17.9 %slice-start = ((s8[7340032]{0:T(1024)(128)(4,1)}), s8[4194304]{0:T(1024)(128)(4,1)S(1)}, s32[]{:S(2)}) async-start(s8[7340032]{0:T(1024)(128)(4,1)} %bitcast.17), calls=%async_computation.1 | async-start | bytes 8388608
  51.8 1.4 %copy-start.4 = (f32[2048,128]{1,0:T(8,128)S(1)}, f32[2048,128]{1,0:T(8,128)}, u32[]{:S(2)}) copy-start(f32[2048,128]{1,0:T(8,128)} %copy-done.3) | copy-start | bytes 3145732
  53.2 16.5 %slice-start.1 = ((s8[7340032]{0:T(1024)(128)(4,1)}), s8[3145728]{0:T(1024)(128)(4,1)S(1)}, s32[]{:S(2)}) async-start(s8[7340032]{0:T(1024)(128)(4,1)} %bitcast.17), calls=%async_computation.2 | async-start | bytes 6291456
  67.7 2.0 %collective-permute-start.11 = (bf16[1024,256]{1,0:T(8,128)(2,1)S(1)}, bf16[1024,256]{1,0:T(8,128)(2,1)S(1)}, u32[]{:S(2)}, u32[]{:S(2)}) collective-permute-start(bf16[1024,256]{1,0:T(8,128)(2,1)S(1)} %get-tuple-element.9), channel_id=1, source_target_pairs={{8,0},{9,1},{10,2},{11,3},{12,4},{13,5},{14,6},{15,7},{0,8},{1,9},... | collective-permute-start | bytes 1572872 | tf_op jit(solution)/shard_map/ppermute | solution.py:303

commit v2 on v0

v2 whole, which is shorter than its diff:
```python
import functools
import itertools
import math

import jax
import jax.numpy as jnp
from jax import lax
from jax.experimental import pallas as pl
from jax.experimental.pallas import tpu as pltpu
from jax.sharding import PartitionSpec as P

NEGATIVE = -1e30
EMPTY = -1e29
AXES = ("blk", "head")
SIZES = (2, 8, 2, 4, 2)
KEYS = 128
DEPTH = 576
PADDED = 640


def linear(place):
    index = 0
    for value, size in zip(place, SIZES):
        index = index * size + value % size
    return index


PLACES = list(itertools.product(*map(range, SIZES)))


def pairs_from(source):
    return [(linear(source(*place)), linear(place)) for place in PLACES]


def side(core):
    return 1 - 2 * core


def fetch(far):
    def source(yh, z, core, x, yl):
        wide = (x + 2 * yl) % 4 // 2
        distance = (3 + wide * (1 - 4 * core)) if far else 1 + wide
        odd = x % 2
        return (yh + odd) % 2, (z + 8 - distance * side(core)) % 8, core, x, (yl + odd) % 2

    return source


def other_core(yh, z, core, x, yl):
    return yh, z, 1 - core, x, yl


def from_x(step):
    return lambda yh, z, core, x, yl: (yh, z, core, (x + 4 - step) % 4, yl)


def from_y(yh, z, core, x, yl):
    return yh, z, core, x, 1 - yl


def start_of(place):
    yh, z, core, _, _ = place
    return [(yh * 8 + z) * 2 + core]


class Shards:
    def __init__(self, array, numbers):
        self.array, self.numbers, self.count = array, numbers, array.shape[0]

    def taken(self, source):
        numbers = self.numbers
        return Shards(lax.ppermute(self.array, AXES, pairs_from(source)), lambda *place: numbers(*source(*place)))

    def joined(self, other):
        a, b = self.numbers, other.numbers
        return Shards(jnp.concatenate([self.array, other.array], 0), lambda *place: a(*place) + b(*place))


def own_place():
    blk, head = lax.axis_index("blk"), lax.axis_index("head")
    return blk // 16, blk // 2 % 8, blk % 2, head // 2, head % 2


def spread():
    return (lax.broadcasted_iota(jnp.int32, (KEYS, KEYS), 0) < 3).astype(jnp.float32).astype(jnp.bfloat16)


def level_of(parts):
    return jnp.dot(parts, spread(), preferred_element_type=jnp.float32)


def attend(queries, group, limits, own, value_weight):
    heads = value_weight.shape[0]
    rows = heads * KEYS
    shards = sum(g.count for g in group)
    first = int(own is not None)
    chunk = 4
    slots = 64
    sub = heads * slots
    scale = (128 + 64) ** -0.5 * math.log2(math.e)
    operands = [*limits, *queries, value_weight, *(g.array for g in group), *(own or ())]

    def kernel(*refs):
        refs = list(refs)
        limit_refs = [refs.pop(0) for _ in range(2)]
        query_refs = [refs.pop(0) for _ in queries]
        weight_ref = refs.pop(0)
        group_refs = [refs.pop(0) for _ in group]
        own_refs = [refs.pop(0) for _ in range(2)] if first else []
        out_refs = [refs.pop(0) for _ in range(2)]
        if first:
            query, table, weight, latents, levels, content, wide, rotary, absorbed, sems = refs
        else:
            table, weight, latents, levels, query, sems = refs
        copies = []

        def copy(start, end):
            made = pltpu.make_async_copy(start, end, sems.at[len(copies)])
            made.start()
            copies.append(made)

        place = own_place()
        numbers = [n for g in group for n in g.numbers(*place)]
        ranks = [sum((other < n).astype(jnp.int32) for other in numbers if other is not n) for n in numbers]
        if first:
            for ref, end in zip(query_refs, (content.at[0], content.at[1], rotary.at[0], rotary.at[1], absorbed)):
                copy(ref, end)
        else:
            copy(query_refs[0], query)
        for i, rank in enumerate(ranks):
            copy(group_refs[i // 2].at[i % 2], table.at[first + rank, pl.ds(0, DEPTH), :])
        if first:
            copy(own_refs[0], table.at[0, pl.ds(0, 512), :])
            copy(own_refs[1], table.at[0, pl.ds(512, 64), :])
        copy(weight_ref, weight)

        row = lax.broadcasted_iota(jnp.int32, (16, KEYS), 0)
        lane = lax.broadcasted_iota(jnp.int32, (16, KEYS), 1)
        limit = jnp.where(row == 0, limit_refs[0][0], limit_refs[1][0])
        hide = [(0, row == 1)] if first else []
        hide += [(first + rank, (row < 2) & (n * KEYS + lane >= limit)) for n, rank in zip(numbers, ranks)]
        for at, hidden in hide:
            table[at, DEPTH : DEPTH + 16, :] = jnp.where(hidden, NEGATIVE, 0.0).astype(jnp.bfloat16)
            table[at, DEPTH + 16 : PADDED, :] = jnp.zeros((PADDED - DEPTH - 16, KEYS), jnp.bfloat16)
        for made in copies[:-1]:
            made.wait()
        if first:
            lanes = lax.broadcasted_iota(jnp.int32, (KEYS, PADDED - DEPTH), 1)
            for slot in range(2):
                wide[...] = content[slot].astype(jnp.float32)
                for head in range(heads):
                    part = slice(head * KEYS, (head + 1) * KEYS)
                    asked = wide[pl.ds(head, KEYS, stride=heads), :].astype(jnp.bfloat16)
                    latent = jnp.dot(asked, absorbed[head], preferred_element_type=jnp.float32)
                    query[slot, part, 0:512] = latent.astype(jnp.bfloat16)
                    rest = [rotary[slot, head].astype(jnp.float32).T, (lanes == slot).astype(jnp.float32)]
                    query[slot, part, 512:PADDED] = jnp.concatenate(rest, 1).astype(jnp.bfloat16)

        def keys(begin, count, depth):
            return jnp.concatenate([table[at, :depth, :] for at in range(begin, begin + count)], 1)

        def work(slot, blocks, chunks):
            spans = [(0, 1)] * first + [(first + i * chunk, chunk) for i in range(chunks)]
            key = lax.broadcasted_iota(jnp.int32, (sub, KEYS), 1)
            time = lax.broadcasted_iota(jnp.int32, (sub, KEYS), 0) % slots
            held = None
            for block in range(blocks + 1):
                found, top = [], jnp.full((sub, 1), EMPTY, jnp.float32)
                if block < blocks:
                    begin = block * slots
                    asked = jnp.concatenate(
                        [query[slot, head * KEYS + begin : head * KEYS + begin + slots, :] for head in range(heads)], 0
                    )
                total, summed = 0.0, 0.0
                for at, span in enumerate(spans):
                    if block < blocks:
                        scores = jnp.dot(asked, keys(*span, PADDED), preferred_element_type=jnp.float32)
                        if first and at == 0:
                            scores = jnp.where(key <= time + begin, scores, NEGATIVE)
                        found.append(scores)
                        top = jnp.maximum(top, jnp.max(scores, axis=1, keepdims=True))
                    if held is not None:
                        weights = jnp.exp2(held[0][at] * scale - held[1] * scale)
                        total = total + jnp.sum(weights, axis=1, keepdims=True)
                        summed = summed + lax.dot_general(
                            weights.astype(jnp.bfloat16),
                            keys(*span, 512),
                            (((1,), (1,)), ((), ())),
                            preferred_element_type=jnp.float32,
                        )
                if held is not None:
                    seen = total > 0.0
                    total = jnp.where(seen, total, 1.0)
                    latent = (summed * (1.0 / total)).astype(jnp.bfloat16)
                    level = jnp.where(seen, held[1] * scale + jnp.log2(total), NEGATIVE)
                    level = jnp.broadcast_to(level, (sub, KEYS))
                    high = level.astype(jnp.bfloat16).astype(jnp.float32)
                    middle = (level - high).astype(jnp.bfloat16).astype(jnp.float32)
                    low = level - high - middle
                    third = jnp.where(key == 0, high, jnp.where(key == 1, middle, jnp.where(key == 2, low, 0.0)))
                    third = third.astype(jnp.bfloat16)
                    for head in range(heads):
                        part = slice(head * slots, (head + 1) * slots)
                        place = head * KEYS + (block - 1) * slots
                        latents[slot, place : place + slots, :] = latent[part, :]
                        levels[slot, place : place + slots, :] = third[part, :]
                held = found, top

        @pl.loop(0, 2)
        def _(slot):
            offset = jnp.where(slot == 0, limit_refs[0][0], limit_refs[1][0])
            length = jnp.where(slot == 0, limit_refs[0][1], limit_refs[1][1])
            visible = sum((n * KEYS < offset).astype(jnp.int32) for n in numbers)
            needed = (visible + chunk - 1) // chunk
            used = jnp.where(length > slots, 2, 1)

            if not first:

                @pl.when(needed == 0)
                def _():
                    latents[slot, :, :] = jnp.zeros((rows, 512), jnp.bfloat16)
                    lanes = lax.broadcasted_iota(jnp.int32, (rows, KEYS), 1)
                    levels[slot, :, :] = jnp.where(lanes == 0, NEGATIVE, 0.0).astype(jnp.bfloat16)

            for chunks in range(1 - first, shards // chunk + 1):
                for blocks in (1, 2):

                    @pl.when((needed == chunks) & (used == blocks))
                    def _():
                        work(slot, blocks, chunks)

        copies[-1].wait()
        for head in range(heads):
            part = slice(head * KEYS, (head + 1) * KEYS)
            for slot, ref in enumerate(out_refs):
                values = jnp.dot(latents[slot, part, :], weight[head], preferred_element_type=jnp.float32)
                ref[part, :KEYS] = values.astype(jnp.bfloat16)
                ref[part, KEYS:] = levels[slot, part, :]

    smem, hbm, vmem = (pl.BlockSpec(memory_space=s) for s in (pltpu.SMEM, pl.ANY, pltpu.VMEM))
    total_keys = (shards + first) * KEYS
    made_from = [
        pltpu.VMEM((2, rows, KEYS), jnp.bfloat16),
        pltpu.VMEM((rows, KEYS), jnp.float32),
        pltpu.VMEM((2, heads, 64, KEYS), jnp.bfloat16),
        pltpu.VMEM((heads, KEYS, 512), jnp.bfloat16),
    ]
    return pl.pallas_call(
        kernel,
        in_specs=[smem] * 2 + [hbm] * (len(operands) - 2),
        out_specs=[vmem] * (2 + first),
        out_shape=[jax.ShapeDtypeStruct((rows, 2 * KEYS), jnp.bfloat16)] * 2
        + [jax.ShapeDtypeStruct((2, rows, PADDED), jnp.bfloat16)] * first,
        scratch_shapes=[
            pltpu.VMEM((shards + first, PADDED, KEYS), jnp.bfloat16),
            pltpu.VMEM((heads, 512, KEYS), jnp.bfloat16),
            pltpu.VMEM((2, rows, 512), jnp.bfloat16),
            pltpu.VMEM((2, rows, KEYS), jnp.bfloat16),
            *(made_from if first else [pltpu.VMEM((2, rows, PADDED), jnp.bfloat16)]),
            pltpu.SemaphoreType.DMA((len(operands) + shards,)),
        ],
        compiler_params=pltpu.CompilerParams(vmem_limit_bytes=(57 if first else 40) * 2**20),
        cost_estimate=pl.CostEstimate(
            flops=4 * rows * total_keys * (PADDED + 512), bytes_accessed=8 << 20, transcendentals=2 * rows * total_keys
        ),
    )(*operands)


def project(pieces, output_weight, length):
    rows = pieces[0].shape[0]
    heads = rows // KEYS
    width = output_weight.shape[-1]
    tile = 896

    def kernel(length_ref, *refs):
        piece_refs = refs[: len(pieces)]
        weight_ref, out_ref, values = refs[len(pieces) :]

        @pl.when(pl.program_id(0) == 0)
        def _():
            for head in range(heads):
                part = slice(head * KEYS, (head + 1) * KEYS)
                levels = [level_of(ref[part, KEYS:]) for ref in piece_refs]
                top = functools.reduce(jnp.maximum, levels)
                shares = [jnp.exp2(level - top) for level in levels]
                both = functools.reduce(
                    jnp.add, [ref[part, :KEYS].astype(jnp.float32) * s for ref, s in zip(piece_refs, shares)]
                ) / functools.reduce(jnp.add, shares)
                slot = lax.broadcasted_iota(jnp.int32, (KEYS, KEYS), 0)
                values[:, part] = jnp.where(slot < length_ref[0], both, 0.0).astype(jnp.bfloat16)

        out_ref[...] = jnp.dot(values[...], weight_ref[...], preferred_element_type=jnp.float32).astype(jnp.bfloat16)

    return pl.pallas_call(
        kernel,
        grid_spec=pltpu.PrefetchScalarGridSpec(
            num_scalar_prefetch=1,
            grid=(width // tile,),
            in_specs=[pl.BlockSpec(p.shape, lambda i, *_: (0, 0)) for p in pieces]
            + [pl.BlockSpec((rows, tile), lambda i, *_: (0, i))],
            out_specs=pl.BlockSpec((KEYS, tile), lambda i, *_: (0, i)),
            scratch_shapes=[pltpu.VMEM((KEYS, rows), jnp.bfloat16)],
        ),
        out_shape=jax.ShapeDtypeStruct((KEYS, width), jnp.bfloat16),
        compiler_params=pltpu.CompilerParams(vmem_limit_bytes=24 * 2**20),
        cost_estimate=pl.CostEstimate(flops=2 * KEYS * rows * width, bytes_accessed=2 * rows * width, transcendentals=0),
    )(length, *pieces, output_weight)


def body(
    query_content,
    query_rotary,
    prompt_latent,
    prompt_rotary,
    reply_latent,
    reply_rotary,
    key_weight,
    value_weight,
    output_weight,
    lengths,
    offsets,
):
    mine = Shards(jnp.concatenate([prompt_latent, prompt_rotary], 0)[None], lambda *place: start_of(place))
    chip = mine.joined(mine.taken(other_core))
    near, far = chip.taken(fetch(0)), chip.taken(fetch(1))
    ways = (from_x(1), from_x(-1), from_y)
    groups = [[held] + [held.taken(w) for w in ways] for held in (near, far)]

    partner = pairs_from(other_core)
    limits = jnp.concatenate([offsets, lengths])
    limits = limits, lax.ppermute(limits, AXES, partner)
    content = query_content.reshape(-1, query_content.shape[-1])
    rotary = query_rotary[0]
    queries = [content, lax.ppermute(content, AXES, partner), rotary, lax.ppermute(rotary, AXES, partner), key_weight]
    own = reply_latent[0], reply_rotary[0]

    mine_near, sent_near, query = attend(queries, groups[0], limits, own, value_weight)
    mine_far, sent_far = attend([query], groups[1], limits, None, value_weight)
    pieces = [mine_near, mine_far, *(lax.ppermute(sent, AXES, partner) for sent in (sent_near, sent_far))]
    term = project(pieces, output_weight.reshape(-1, output_weight.shape[-1]), lengths)
    parts = lax.all_to_all(term, "head", 0, 0, tiled=True)
    parts = parts.reshape(8, parts.shape[0] // 8, -1).astype(jnp.float32)
    return jnp.sum(parts, 0).astype(jnp.bfloat16)[:, None, :]


def solution(mesh):
    placed = (
        P("blk", None, "head", None),
        P("blk", "head", None, None),
        P(None, "blk"),
        P(None, "blk"),
        P("blk", None, None),
        P("blk", None, None),
        P("head", None, None),
        P("head", None, None),
        P("head", None, None),
        P("blk"),
        P("blk"),
    )
    return jax.shard_map(
        body, mesh=mesh, in_specs=placed, out_specs=P("head", "blk", None), check_vma=False
    )
```

time: 204 us -> 87.6 us (0.43)
  the two profiles are of different devices: /device:TPU:48 before, /device:TPU:1 now
where the time goes in v2:
time: 87.6 us; the launch traced here: 86.6 us
  starting transfers between devices  29.7 us (34%)
  Pallas kernels  28.2 us (32%)
  blocking collectives  18 us (21%)
  local copies, waits for them, and re-layouts  3.86 us (4%)
  waiting for transfers between devices  3.55 us (4%)
  other arithmetic  1.82 us (2%)
  between operations  1.49 us (2%)
    ppermute x9, starting transfers between devices, taken(): lax.ppermute(self.array, AXES, pairs_from(source))  27.5 us
    pallas_call x2, Pallas kernels, attend(): pl.pallas_call(kernel, in_specs=[smem] * 2 + [hbm] * (len(operands) - 2),...  25 us
    all_to_all x1, blocking collectives, body(): parts = lax.all_to_all(term, 'head', 0, 0, tiled=True)  18 us
    unnamed x30, local copies, waits for them, and re-layouts  3.86 us
    pallas_call x1, Pallas kernels, project(): pl.pallas_call(kernel, grid_spec=pltpu.PrefetchScalarGridSpec(num_scalar_...  3.25 us
    ppermute x2, waiting for transfers between devices, body(): lax.ppermute(sent, AXES, partner)  2.18 us
    ppermute x2, starting transfers between devices, body(): lax.ppermute(sent, AXES, partner)  1.78 us
  transfers between devices with their start and end apart: 14, of which 4 were waited for; matrix products, arithmetic and copies ran while one was open for 0% of the time, Pallas kernels for 17%

profile of v2, /device:TPU:1, one launch (start us, length us, event | category | flops | bytes accessed | tf_op | source)
XLA Modules:
  0.0 86.6 jit_solution(8051081124814531395)
XLA Ops:
  0.0 0.9 %maximum_bitcast_fusion = bf16[1,576,128]{2,1,0:T(8,128)(2,1)S(1)} fusion(bf16[64,128]{1,0:T(8,128)(2,1)} %param.14, bf16[512,128]{1,0:T(8,128)(2,1)} %param.13), kind=kLoop, calls=%fused_computation.1 | loop fusion | flops 294912 | bytes 294912 | tf_op jit(solution)/shard_map/broadcast_in_dim | solution.py:323
  0.9 3.3 %collective-permute-start.3 = (bf16[1,576,128]{2,1,0:T(8,128)(2,1)S(1)}, bf16[1,576,128]{2,1,0:T(8,128)(2,1)S(1)}, u32[]{:S(2)}, u32[]{:S(2)}) collective-permute-start(bf16[1,576,128]{2,1,0:T(8,128)(2,1)S(1)} %maximum_bitcast_fusion), channel_id=1, source_target_pairs={{8,0},{9,1},{10,2},{11,3},{12,4},{13,5},{14,6},{15,7},{0,8},{1,9},... | collective-permute-start | bytes 442376 | tf_op jit(solution)/shard_map/ppermute | solution.py:72
  4.3 1.0 %collective-permute-done.3 = bf16[1,576,128]{2,1,0:T(8,128)(2,1)S(1)} collective-permute-done((bf16[1,576,128]{2,1,0:T(8,128)(2,1)S(1)}, bf16[1,576,128]{2,1,0:T(8,128)(2,1)S(1)}, u32[]{:S(2)}, u32[]{:S(2)}) %collective-permute-start.3) | collective-permute-done | bytes 147488 | tf_op jit(solution)/shard_map/ppermute | solution.py:72
  5.3 3.9 %collective-permute-start.4 = (bf16[2,576,128]{2,1,0:T(8,128)(2,1)S(1)}, bf16[2,576,128]{2,1,0:T(8,128)(2,1)S(1)}, u32[]{:S(2)}, u32[]{:S(2)}) collective-permute-start(bf16[2,576,128]{2,1,0:T(8,128)(2,1)S(1)} %pad_maximum_fusion), channel_id=1, source_target_pairs={{112,0},{97,1},{243,2},{226,3},{100,4},{117,5},{231,6},{246,7},{24... | collective-permute-start | bytes 884744 | tf_op jit(solution)/shard_map/ppermute | solution.py:72
  9.2 0.0 collective-permute-start.2
  10.5 4.2 %collective-permute-start.8 = (bf16[2,576,128]{2,1,0:T(8,128)(2,1)S(1)}, bf16[2,576,128]{2,1,0:T(8,128)(2,1)S(1)}, u32[]{:S(2)}, u32[]{:S(2)}) collective-permute-start(bf16[2,576,128]{2,1,0:T(8,128)(2,1)S(1)} %pad_maximum_fusion), channel_id=1, source_target_pairs={{80,0},{65,1},{211,2},{194,3},{68,4},{85,5},{199,6},{214,7},{56,8}... | collective-permute-start | bytes 884744 | tf_op jit(solution)/shard_map/ppermute | solution.py:72
  14.7 0.1 pad_add_fusion.refs_0_
  14.8 0.0 copy-start.3
  14.8 0.3 collective-permute-start
  15.1 0.0 collective-permute-done.4.refs_8_
  15.1 0.0 copy-start.9
  15.1 9.6 %collective-permute-start.5 = (bf16[2,576,128]{2,1,0:T(8,128)(2,1)S(1)}, bf16[2,576,128]{2,1,0:T(8,128)(2,1)S(1)}, u32[]{:S(2)}, u32[]{:S(2)}) collective-permute-start(bf16[2,576,128]{2,1,0:T(8,128)(2,1)S(1)} %collective-permute-done.4.refs_8_), channel_id=1, source_target_pairs={{6,0},{7,1},{0,2},{1,3},{2,4},{3,5},{4,6},{5,7},{14,8},{15,9},{8,1... | collective-permute-start | bytes 884744 | tf_op jit(solution)/shard_map/ppermute | solution.py:72
  24.7 0.0 collective-permute-start.6
  24.7 0.0 collective-permute-done.refs_1_
  24.7 0.0 copy-start.5
  24.7 0.1 collective-permute-start.7
  24.8 0.0 collective-permute-done.2.refs_5_
  24.8 0.0 copy-start.14
  24.8 0.1 collective-permute-start.1
  24.9 0.3 collective-permute-done.8.refs_4_
  25.3 3.4 %collective-permute-start.10 = (bf16[2,576,128]{2,1,0:T(8,128)(2,1)S(1)}, bf16[2,576,128]{2,1,0:T(8,128)(2,1)S(1)}, u32[]{:S(2)}, u32[]{:S(2)}) collective-permute-start(bf16[2,576,128]{2,1,0:T(8,128)(2,1)S(1)} %collective-permute-done.8.refs_4_), channel_id=1, source_target_pairs={{2,0},{3,1},{4,2},{5,3},{6,4},{7,5},{0,6},{1,7},{10,8},{11,9},{12,... | collective-permute-start | bytes 884744 | tf_op jit(solution)/shard_map/ppermute | solution.py:72
  28.7 0.0 collective-permute-done.1.refs_3_
  28.7 0.0 copy-start.13
  28.7 2.7 %collective-permute-start.11 = (bf16[2,576,128]{2,1,0:T(8,128)(2,1)S(1)}, bf16[2,576,128]{2,1,0:T(8,128)(2,1)S(1)}, u32[]{:S(2)}, u32[]{:S(2)}) collective-permute-start(bf16[2,576,128]{2,1,0:T(8,128)(2,1)S(1)} %collective-permute-done.8.refs_4_), channel_id=1, source_target_pairs={{1,0},{0,1},{3,2},{2,3},{5,4},{4,5},{7,6},{6,7},{9,8},{8,9},{11,10... | collective-permute-start | bytes 884744 | tf_op jit(solution)/shard_map/ppermute | solution.py:72
  31.4 0.0 collective-permute-done.5.refs_9_
  31.4 0.0 copy-start.10
  31.4 0.3 collective-permute-start.9
  31.7 0.0 collective-permute-done.6.refs_10_
  31.7 0.0 copy-start.11
  31.7 0.0 collective-permute-done.7.refs_11_
  31.7 0.0 copy-start.12
  31.7 0.0 copy-done.3
  31.7 0.0 copy-done.9
  31.7 0.0 copy-done.5
  31.7 0.0 copy-done.14
  31.7 0.0 copy-done.13
  31.8 0.4 copy-done.10
  32.1 0.3 copy-done.11
  32.4 0.1 copy-done.12
  32.5 0.0 copy-start.2
  32.5 14.3 %shard_map.109 = (bf16[1024,256]{1,0:T(8,128)(2,1)}, bf16[1024,256]{1,0:T(8,128)(2,1)}, bf16[2,1024,640]{2,1,0:T(8,128)(2,1)}) custom-call(s32[2]{0:T(128)} %copy-done.3, s32[2]{0:T(128)} %copy-done.5, bf16[1024,128]{1,0:T(8,128)(2,1)} %bitcast.12, bf16[1024,128]{1,0:T(8,128)(2,1)} %copy-done.13, bf16[8,64,128]{2,1,0:T(8,128)(2,1)} %bitcast.14, ...), custom_call_target="tpu_custom_call" | custom-call | flops 5435817984 | bytes 8388608 | tf_op jit(solution)/shard_map/pallas_call | solution.py:248
  46.9 0.0 collective-permute-done.10.refs_6_
  46.9 0.0 collective-permute-done.11.refs_7_
  46.9 0.0 collective-permute-done.9.refs_5_
  46.9 0.0 copy-done.2
  46.9 0.0 copy-start.4
  46.9 0.6 copy-done.4
  47.6 0.0 copy-start.6
  47.6 0.7 copy-done.6
  48.2 0.0 copy-start.7
  48.2 1.7 %copy-done.7 = bf16[2,1024,640]{2,1,0:T(8,128)(2,1)S(1)} copy-done((bf16[2,1024,640]{2,1,0:T(8,128)(2,1)S(1)}, bf16[2,1024,640]{2,1,0:T(8,128)(2,1)}, u32[]{:S(2)}) %copy-start.7) | copy-done | bytes 2621464
  50.0 0.0 copy-start.8
  50.0 0.0 copy-start
  50.0 10.6 %shard_map.110 = (bf16[1024,256]{1,0:T(8,128)(2,1)S(1)}, bf16[1024,256]{1,0:T(8,128)(2,1)S(1)}) custom-call(s32[2]{0:T(128)S(1)} %copy-done.4, s32[2]{0:T(128)S(1)} %copy-done.6, bf16[2,1024,640]{2,1,0:T(8,128)(2,1)S(1)} %copy-done.7, bf16[8,512,128]{2,1,0:T(8,128)(2,1)S(1)} %copy-done.2, bf16[2,576,128]{2,1,0:T(8,128)(2,1)S(1)} %collective-permute-done.8.refs_4_, ...), custom_call_target="tpu_custom_call" | custom-call | flops 4831838208 | bytes 8388608 | tf_op jit(solution)/shard_map/pallas_call | solution.py:248
  60.6 1.7 %collective-permute-start.13 = (bf16[1024,256]{1,0:T(8,128)(2,1)S(1)}, bf16[1024,256]{1,0:T(8,128)(2,1)S(1)}, u32[]{:S(2)}, u32[]{:S(2)}) collective-permute-start(bf16[1024,256]{1,0:T(8,128)(2,1)S(1)} %get-tuple-element.14), channel_id=1, source_target_pairs={{8,0},{9,1},{10,2},{11,3},{12,4},{13,5},{14,6},{15,7},{0,8},{1,9},... | collective-permute-start | bytes 1572872 | tf_op jit(solution)/shard_map/ppermute | solution.py:339
  62.3 0.0 copy-done.8
  62.3 0.1 collective-permute-start.12
  62.4 1.4 %collective-permute-done.13.refs_3_ = bf16[1024,256]{1,0:T(8,128)(2,1)S(1)} collective-permute-done((bf16[1024,256]{1,0:T(8,128)(2,1)S(1)}, bf16[1024,256]{1,0:T(8,128)(2,1)S(1)}, u32[]{:S(2)}, u32[]{:S(2)}) %collective-permute-start.13) | collective-permute-done | bytes 524320 | tf_op jit(solution)/shard_map/ppermute | solution.py:339
  63.8 0.7 collective-permute-done.12.refs_2_
  64.6 0.0 copy-done
  64.6 0.0 copy-done.1
  64.6 3.3 %shard_map.111 = bf16[128,3584]{1,0:T(8,128)(2,1)S(1)} custom-call(s32[1]{0:T(128)S(6)} %copy.12.length_ref, bf16[1024,256]{1,0:T(8,128)(2,1)S(1)} %copy-done.1, bf16[1024,256]{1,0:T(8,128)(2,1)S(1)} %get-tuple-element.12.refs_1_, bf16[1024,256]{1,0:T(8,128)(2,1)S(1)} %collective-permute-done.12.refs_2_, ...), custom_call_target="tpu_custom_call" | custom-call | flops 939524096 | bytes 7340032 | tf_op jit(solution)/shard_map/pallas_call | solution.py:294
  67.9 18.0 %all_to_all.9 = bf16[8,16,3584]{2,1,0:T(8,128)(2,1)S(1)} all-to-all(bf16[8,16,3584]{2,1,0:T(8,128)(2,1)S(1)} %bitcast.10), channel_id=1, replica_groups=mesh['blk'=32,'head'=8] {'head'}, dimensions={0} | all-to-all | bytes 1835008 | tf_op jit(solution)/shard_map/all_to_all | solution.py:341
  85.8 0.8 reduce_sum.12
  (2 shorter events, 0.0 us)
Async XLA Ops:
  0.9 4.3 %collective-permute-start.3 = (bf16[1,576,128]{2,1,0:T(8,128)(2,1)S(1)}, bf16[1,576,128]{2,1,0:T(8,128)(2,1)S(1)}, u32[]{:S(2)}, u32[]{:S(2)}) collective-permute-start(bf16[1,576,128]{2,1,0:T(8,128)(2,1)S(1)} %maximum_bitcast_fusion), channel_id=1, source_target_pairs={{8,0},{9,1},{10,2},{11,3},{12,4},{13,5},{14,6},{15,7},{0,8},{1,9},... | collective-permute-start | bytes 442376 | tf_op jit(solution)/shard_map/ppermute | solution.py:72
  5.3 9.8 %collective-permute-start.4 = (bf16[2,576,128]{2,1,0:T(8,128)(2,1)S(1)}, bf16[2,576,128]{2,1,0:T(8,128)(2,1)S(1)}, u32[]{:S(2)}, u32[]{:S(2)}) collective-permute-start(bf16[2,576,128]{2,1,0:T(8,128)(2,1)S(1)} %pad_maximum_fusion), channel_id=1, source_target_pairs={{112,0},{97,1},{243,2},{226,3},{100,4},{117,5},{231,6},{246,7},{24... | collective-permute-start | bytes 884744 | tf_op jit(solution)/shard_map/ppermute | solution.py:72
  9.2 15.6 %collective-permute-start.2 = (bf16[8,64,128]{2,1,0:T(8,128)(2,1)}, bf16[8,64,128]{2,1,0:T(8,128)(2,1)S(1)}, u32[]{:S(2)}, u32[]{:S(2)}) collective-permute-start(bf16[8,64,128]{2,1,0:T(8,128)(2,1)} %bitcast.13), channel_id=1, source_target_pairs={{8,0},{9,1},{10,2},{11,3},{12,4},{13,5},{14,6},{15,7},{0,8},{1,9},... | collective-permute-start | bytes 393224 | tf_op jit(solution)/shard_map/ppermute | solution.py:334
  10.5 14.8 %collective-permute-start.8 = (bf16[2,576,128]{2,1,0:T(8,128)(2,1)S(1)}, bf16[2,576,128]{2,1,0:T(8,128)(2,1)S(1)}, u32[]{:S(2)}, u32[]{:S(2)}) collective-permute-start(bf16[2,576,128]{2,1,0:T(8,128)(2,1)S(1)} %pad_maximum_fusion), channel_id=1, source_target_pairs={{80,0},{65,1},{211,2},{194,3},{68,4},{85,5},{199,6},{214,7},{56,8}... | collective-permute-start | bytes 884744 | tf_op jit(solution)/shard_map/ppermute | solution.py:72
  14.8 16.9 %copy-start.3 = (s32[2]{0:T(128)}, s32[2]{0:T(128)S(1)}, u32[]{:S(2)}) copy-start(s32[2]{0:T(128)S(1)} %pad_add_fusion.refs_0_) | copy-start | bytes 28
  14.8 9.9 %collective-permute-start = (s32[2]{0:T(128)S(1)}, s32[2]{0:T(128)S(1)}, u32[]{:S(2)}, u32[]{:S(2)}) collective-permute-start(s32[2]{0:T(128)S(1)} %pad_add_fusion.refs_0_), channel_id=1, source_target_pairs={{8,0},{9,1},{10,2},{11,3},{12,4},{13,5},{14,6},{15,7},{0,8},{1,9},... | collective-permute-start | bytes 32 | tf_op jit(solution)/shard_map/ppermute | solution.py:331
  15.1 16.6 %copy-start.9 = (bf16[2,576,128]{2,1,0:T(8,128)(2,1)}, bf16[2,576,128]{2,1,0:T(8,128)(2,1)S(1)}, u32[]{:S(2)}) copy-start(bf16[2,576,128]{2,1,0:T(8,128)(2,1)S(1)} %collective-permute-done.4.refs_8_) | copy-start | bytes 884740
  15.1 16.3 %collective-permute-start.5 = (bf16[2,576,128]{2,1,0:T(8,128)(2,1)S(1)}, bf16[2,576,128]{2,1,0:T(8,128)(2,1)S(1)}, u32[]{:S(2)}, u32[]{:S(2)}) collective-permute-start(bf16[2,576,128]{2,1,0:T(8,128)(2,1)S(1)} %collective-permute-done.4.refs_8_), channel_id=1, source_target_pairs={{6,0},{7,1},{0,2},{1,3},{2,4},{3,5},{4,6},{5,7},{14,8},{15,9},{8,1... | collective-permute-start | bytes 884744 | tf_op jit(solution)/shard_map/ppermute | solution.py:72
  24.7 7.0 %collective-permute-start.6 = (bf16[2,576,128]{2,1,0:T(8,128)(2,1)S(1)}, bf16[2,576,128]{2,1,0:T(8,128)(2,1)S(1)}, u32[]{:S(2)}, u32[]{:S(2)}) collective-permute-start(bf16[2,576,128]{2,1,0:T(8,128)(2,1)S(1)} %collective-permute-done.4.refs_8_), channel_id=1, source_target_pairs={{2,0},{3,1},{4,2},{5,3},{6,4},{7,5},{0,6},{1,7},{10,8},{11,9},{12,... | collective-permute-start | bytes 884744 | tf_op jit(solution)/shard_map/ppermute | solution.py:72
  24.7 7.0 %copy-start.5 = (s32[2]{0:T(128)}, s32[2]{0:T(128)S(1)}, u32[]{:S(2)}) copy-start(s32[2]{0:T(128)S(1)} %collective-permute-done.refs_1_) | copy-start | bytes 28
  24.7 7.0 %collective-permute-start.7 = (bf16[2,576,128]{2,1,0:T(8,128)(2,1)S(1)}, bf16[2,576,128]{2,1,0:T(8,128)(2,1)S(1)}, u32[]{:S(2)}, u32[]{:S(2)}) collective-permute-start(bf16[2,576,128]{2,1,0:T(8,128)(2,1)S(1)} %collective-permute-done.4.refs_8_), channel_id=1, source_target_pairs={{1,0},{0,1},{3,2},{2,3},{5,4},{4,5},{7,6},{6,7},{9,8},{8,9},{11,10... | collective-permute-start | bytes 884744 | tf_op jit(solution)/shard_map/ppermute | solution.py:72
  24.8 6.9 %copy-start.14 = (bf16[8,64,128]{2,1,0:T(8,128)(2,1)}, bf16[8,64,128]{2,1,0:T(8,128)(2,1)S(1)}, u32[]{:S(2)}) copy-start(bf16[8,64,128]{2,1,0:T(8,128)(2,1)S(1)} %collective-permute-done.2.refs_5_) | copy-start | bytes 393220
  24.8 3.9 %collective-permute-start.1 = (bf16[1024,128]{1,0:T(8,128)(2,1)}, bf16[1024,128]{1,0:T(8,128)(2,1)S(1)}, u32[]{:S(2)}, u32[]{:S(2)}) collective-permute-start(bf16[1024,128]{1,0:T(8,128)(2,1)} %bitcast.11), channel_id=1, source_target_pairs={{8,0},{9,1},{10,2},{11,3},{12,4},{13,5},{14,6},{15,7},{0,8},{1,9},... | collective-permute-start | bytes 786440 | tf_op jit(solution)/shard_map/ppermute | solution.py:334
  25.3 21.6 %collective-permute-start.10 = (bf16[2,576,128]{2,1,0:T(8,128)(2,1)S(1)}, bf16[2,576,128]{2,1,0:T(8,128)(2,1)S(1)}, u32[]{:S(2)}, u32[]{:S(2)}) collective-permute-start(bf16[2,576,128]{2,1,0:T(8,128)(2,1)S(1)} %collective-permute-done.8.refs_4_), channel_id=1, source_target_pairs={{2,0},{3,1},{4,2},{5,3},{6,4},{7,5},{0,6},{1,7},{10,8},{11,9},{12,... | collective-permute-start | bytes 884744 | tf_op jit(solution)/shard_map/ppermute | solution.py:72
  28.7 3.0 %copy-start.13 = (bf16[1024,128]{1,0:T(8,128)(2,1)}, bf16[1024,128]{1,0:T(8,128)(2,1)S(1)}, u32[]{:S(2)}) copy-start(bf16[1024,128]{1,0:T(8,128)(2,1)S(1)} %collective-permute-done.1.refs_3_) | copy-start | bytes 786436
  28.7 18.1 %collective-permute-start.11 = (bf16[2,576,128]{2,1,0:T(8,128)(2,1)S(1)}, bf16[2,576,128]{2,1,0:T(8,128)(2,1)S(1)}, u32[]{:S(2)}, u32[]{:S(2)}) collective-permute-start(bf16[2,576,128]{2,1,0:T(8,128)(2,1)S(1)} %collective-permute-done.8.refs_4_), channel_id=1, source_target_pairs={{1,0},{0,1},{3,2},{2,3},{5,4},{4,5},{7,6},{6,7},{9,8},{8,9},{11,10... | collective-permute-start | bytes 884744 | tf_op jit(solution)/shard_map/ppermute | solution.py:72
  31.4 0.7 copy-start.10
  31.4 15.5 %collective-permute-start.9 = (bf16[2,576,128]{2,1,0:T(8,128)(2,1)S(1)}, bf16[2,576,128]{2,1,0:T(8,128)(2,1)S(1)}, u32[]{:S(2)}, u32[]{:S(2)}) collective-permute-start(bf16[2,576,128]{2,1,0:T(8,128)(2,1)S(1)} %collective-permute-done.8.refs_4_), channel_id=1, source_target_pairs={{6,0},{7,1},{0,2},{1,3},{2,4},{3,5},{4,6},{5,7},{14,8},{15,9},{8,1... | collective-permute-start | bytes 884744 | tf_op jit(solution)/shard_map/ppermute | solution.py:72
  31.7 0.7 copy-start.11
  31.7 0.8 copy-start.12
  32.5 14.4 %copy-start.2 = (bf16[8,512,128]{2,1,0:T(8,128)(2,1)S(1)}, bf16[8,512,128]{2,1,0:T(8,128)(2,1)}, u32[]{:S(2)}) copy-start(bf16[8,512,128]{2,1,0:T(8,128)(2,1)} %refs_3_.1) | copy-start | bytes 3145732
  46.9 0.7 copy-start.4
  47.6 0.7 copy-start.6
  48.2 1.7 %copy-start.7 = (bf16[2,1024,640]{2,1,0:T(8,128)(2,1)S(1)}, bf16[2,1024,640]{2,1,0:T(8,128)(2,1)}, u32[]{:S(2)}) copy-start(bf16[2,1024,640]{2,1,0:T(8,128)(2,1)} %get-tuple-element.11.refs_2_) | copy-start | bytes 7864324
  50.0 12.3 %copy-start.8 = (bf16[1024,256]{1,0:T(8,128)(2,1)S(1)}, bf16[1024,256]{1,0:T(8,128)(2,1)}, u32[]{:S(2)}) copy-start(bf16[1024,256]{1,0:T(8,128)(2,1)} %get-tuple-element.13) | copy-start | bytes 1572868
  50.0 14.6 %copy-start = (bf16[8,128,3584]{2,1,0:T(8,128)(2,1)S(1)}, bf16[8,128,3584]{2,1,0:T(8,128)(2,1)}, u32[]{:S(2)}) copy-start(bf16[8,128,3584]{2,1,0:T(8,128)(2,1)} %param.19) | copy-start | bytes 22020100
  50.0 14.6 %copy-start.1 = (bf16[1024,256]{1,0:T(8,128)(2,1)S(1)}, bf16[1024,256]{1,0:T(8,128)(2,1)}, u32[]{:S(2)}) copy-start(bf16[1024,256]{1,0:T(8,128)(2,1)} %get-tuple-element.10.refs_0_) | copy-start | bytes 1572868
  60.6 3.2 %collective-permute-start.13 = (bf16[1024,256]{1,0:T(8,128)(2,1)S(1)}, bf16[1024,256]{1,0:T(8,128)(2,1)S(1)}, u32[]{:S(2)}, u32[]{:S(2)}) collective-permute-start(bf16[1024,256]{1,0:T(8,128)(2,1)S(1)} %get-tuple-element.14), channel_id=1, source_target_pairs={{8,0},{9,1},{10,2},{11,3},{12,4},{13,5},{14,6},{15,7},{0,8},{1,9},... | collective-permute-start | bytes 1572872 | tf_op jit(solution)/shard_map/ppermute | solution.py:339
  62.3 2.3 %collective-permute-start.12 = (bf16[1024,256]{1,0:T(8,128)(2,1)S(1)}, bf16[1024,256]{1,0:T(8,128)(2,1)S(1)}, u32[]{:S(2)}, u32[]{:S(2)}) collective-permute-start(bf16[1024,256]{1,0:T(8,128)(2,1)S(1)} %copy-done.8), channel_id=1, source_target_pairs={{8,0},{9,1},{10,2},{11,3},{12,4},{13,5},{14,6},{15,7},{0,8},{1,9},... | collective-permute-start | bytes 1572872 | tf_op jit(solution)/shard_map/ppermute | solution.py:339

commit v3 on v2

--- a/solution.py
+++ b/solution.py
@@ -89,7 +89,16 @@
     return jnp.dot(parts, spread(), preferred_element_type=jnp.float32)
 
 
-def attend(queries, group, limits, own, value_weight):
+def in_thirds(level):
+    lane = lax.broadcasted_iota(jnp.int32, level.shape, 1)
+    high = level.astype(jnp.bfloat16).astype(jnp.float32)
+    middle = (level - high).astype(jnp.bfloat16).astype(jnp.float32)
+    low = level - high - middle
+    parts = jnp.where(lane == 0, high, jnp.where(lane == 1, middle, jnp.where(lane == 2, low, 0.0)))
+    return parts.astype(jnp.bfloat16)
+
+
+def attend(queries, group, limits, own, before, value_weight):
     heads = value_weight.shape[0]
     rows = heads * KEYS
     shards = sum(g.count for g in group)
@@ -98,7 +107,7 @@
     slots = 64
     sub = heads * slots
     scale = (128 + 64) ** -0.5 * math.log2(math.e)
-    operands = [*limits, *queries, value_weight, *(g.array for g in group), *(own or ())]
+    operands = [*limits, *queries, value_weight, *(g.array for g in group), *(own or before)]
 
     def kernel(*refs):
         refs = list(refs)
@@ -106,12 +115,12 @@
         query_refs = [refs.pop(0) for _ in queries]
         weight_ref = refs.pop(0)
         group_refs = [refs.pop(0) for _ in group]
-        own_refs = [refs.pop(0) for _ in range(2)] if first else []
+        own_refs = [refs.pop(0) for _ in range(2)]
         out_refs = [refs.pop(0) for _ in range(2)]
         if first:
             query, table, weight, latents, levels, content, wide, rotary, absorbed, sems = refs
         else:
-            table, weight, latents, levels, query, sems = refs
+            table, weight, latents, levels, query, earlier, sems = refs
         copies = []
 
         def copy(start, end):
@@ -132,6 +141,9 @@
         if first:
             copy(own_refs[0], table.at[0, pl.ds(0, 512), :])
             copy(own_refs[1], table.at[0, pl.ds(512, 64), :])
+        else:
+            copy(own_refs[0], earlier.at[0])
+            copy(own_refs[1], earlier.at[1])
         copy(weight_ref, weight)
 
         row = lax.broadcasted_iota(jnp.int32, (16, KEYS), 0)
@@ -142,7 +154,7 @@
         for at, hidden in hide:
             table[at, DEPTH : DEPTH + 16, :] = jnp.where(hidden, NEGATIVE, 0.0).astype(jnp.bfloat16)
             table[at, DEPTH + 16 : PADDED, :] = jnp.zeros((PADDED - DEPTH - 16, KEYS), jnp.bfloat16)
-        for made in copies[:-1]:
+        for made in copies[: len(queries)]:
             made.wait()
         if first:
             lanes = lax.broadcasted_iota(jnp.int32, (KEYS, PADDED - DEPTH), 1)
@@ -155,6 +167,9 @@
                     query[slot, part, 0:512] = latent.astype(jnp.bfloat16)
                     rest = [rotary[slot, head].astype(jnp.float32).T, (lanes == slot).astype(jnp.float32)]
                     query[slot, part, 512:PADDED] = jnp.concatenate(rest, 1).astype(jnp.bfloat16)
+        late = 1 if first else 3
+        for made in copies[len(queries) : -late]:
+            made.wait()
 
         def keys(begin, count, depth):
             return jnp.concatenate([table[at, :depth, :] for at in range(begin, begin + count)], 1)
@@ -194,11 +209,7 @@
                     latent = (summed * (1.0 / total)).astype(jnp.bfloat16)
                     level = jnp.where(seen, held[1] * scale + jnp.log2(total), NEGATIVE)
                     level = jnp.broadcast_to(level, (sub, KEYS))
-                    high = level.astype(jnp.bfloat16).astype(jnp.float32)
-                    middle = (level - high).astype(jnp.bfloat16).astype(jnp.float32)
-                    low = level - high - middle
-                    third = jnp.where(key == 0, high, jnp.where(key == 1, middle, jnp.where(key == 2, low, 0.0)))
-                    third = third.astype(jnp.bfloat16)
+                    third = in_thirds(level)
                     for head in range(heads):
                         part = slice(head * slots, (head + 1) * slots)
                         place = head * KEYS + (block - 1) * slots
@@ -229,13 +240,24 @@
                     def _():
                         work(slot, blocks, chunks)
 
-        copies[-1].wait()
+        for made in copies[-late:]:
+            made.wait()
         for head in range(heads):
             part = slice(head * KEYS, (head + 1) * KEYS)
+            both = jnp.concatenate([latents[slot, part, :] for slot in range(2)], 0)
+            both = jnp.dot(both, weight[head], preferred_element_type=jnp.float32)
             for slot, ref in enumerate(out_refs):
-                values = jnp.dot(latents[slot, part, :], weight[head], preferred_element_type=jnp.float32)
+                values = both[slot * KEYS : (slot + 1) * KEYS, :]
+                if first:
+                    ref[part, :KEYS] = values.astype(jnp.bfloat16)
+                    ref[part, KEYS:] = levels[slot, part, :]
+                    continue
+                one, two = level_of(earlier[slot, part, KEYS:]), level_of(levels[slot, part, :])
+                top = jnp.maximum(one, two)
+                a, b = jnp.exp2(one - top), jnp.exp2(two - top)
+                values = (earlier[slot, part, :KEYS].astype(jnp.float32) * a + values * b) / (a + b)
                 ref[part, :KEYS] = values.astype(jnp.bfloat16)
-                ref[part, KEYS:] = levels[slot, part, :]
+                ref[part, KEYS:] = in_thirds(top + jnp.log2(a + b))
 
     smem, hbm, vmem = (pl.BlockSpec(memory_space=s) for s in (pltpu.SMEM, pl.ANY, pltpu.VMEM))
     total_keys = (shards + first) * KEYS
@@ -256,10 +278,10 @@
             pltpu.VMEM((heads, 512, KEYS), jnp.bfloat16),
             pltpu.VMEM((2, rows, 512), jnp.bfloat16),
             pltpu.VMEM((2, rows, KEYS), jnp.bfloat16),
-            *(made_from if first else [pltpu.VMEM((2, rows, PADDED), jnp.bfloat16)]),
+            *(made_from if first else [pltpu.VMEM((2, rows, PADDED), jnp.bfloat16), pltpu.VMEM((2, rows, 2 * KEYS), jnp.bfloat16)]),
             pltpu.SemaphoreType.DMA((len(operands) + shards,)),
         ],
-        compiler_params=pltpu.CompilerParams(vmem_limit_bytes=(57 if first else 40) * 2**20),
+        compiler_params=pltpu.CompilerParams(vmem_limit_bytes=(57 if first else 52) * 2**20),
         cost_estimate=pl.CostEstimate(
             flops=4 * rows * total_keys * (PADDED + 512), bytes_accessed=8 << 20, transcendentals=2 * rows * total_keys
         ),
@@ -334,9 +356,9 @@
     queries = [content, lax.ppermute(content, AXES, partner), rotary, lax.ppermute(rotary, AXES, partner), key_weight]
     own = reply_latent[0], reply_rotary[0]
 
-    mine_near, sent_near, query = attend(queries, groups[0], limits, own, value_weight)
-    mine_far, sent_far = attend([query], groups[1], limits, None, value_weight)
-    pieces = [mine_near, mine_far, *(lax.ppermute(sent, AXES, partner) for sent in (sent_near, sent_far))]
+    *pieces, query = attend(queries, groups[0], limits, own, None, value_weight)
+    mine_part, sent = attend([query], groups[1], limits, None, pieces, value_weight)
+    pieces = mine_part, lax.ppermute(sent, AXES, partner)
     term = project(pieces, output_weight.reshape(-1, output_weight.shape[-1]), lengths)
     parts = lax.all_to_all(term, "head", 0, 0, tiled=True)
     parts = parts.reshape(8, parts.shape[0] // 8, -1).astype(jnp.float32)

time: 87.6 us -> 83.3 us (0.951)
  the two profiles are of different devices: /device:TPU:1 before, /device:TPU:48 now
where the time goes in v3:
time: 83.3 us; the launch traced here: 83.8 us
  Pallas kernels  27.1 us (33%)
  starting transfers between devices  26.2 us (31%)
  blocking collectives  18.7 us (22%)
  waiting for transfers between devices  6.33 us (8%)
  local copies, waits for them, and re-layouts  2.18 us (3%)
  other arithmetic  1.82 us (2%)
  between operations  1.48 us (2%)
    ppermute x9, starting transfers between devices, taken(): lax.ppermute(self.array, AXES, pairs_from(source))  25.9 us
    pallas_call x2, Pallas kernels, attend(): pl.pallas_call(kernel, in_specs=[smem] * 2 + [hbm] * (len(operands) - 2),...  24.2 us
    all_to_all x1, blocking collectives, body(): parts = lax.all_to_all(term, 'head', 0, 0, tiled=True)  18.7 us
    ppermute x9, waiting for transfers between devices, taken(): lax.ppermute(self.array, AXES, pairs_from(source))  4.22 us
    pallas_call x1, Pallas kernels, project(): pl.pallas_call(kernel, grid_spec=pltpu.PrefetchScalarGridSpec(num_scalar_...  2.93 us
    unnamed x22, local copies, waits for them, and re-layouts  2.18 us
    ppermute x1, waiting for transfers between devices, body(): pieces = (mine_part, lax.ppermute(sent, AXES, partner))  2.11 us
  transfers between devices with their start and end apart: 13, of which 3 were waited for; matrix products, arithmetic and copies ran while one was open for 0% of the time, Pallas kernels for 16%

profile of v3, /device:TPU:48, one launch (start us, length us, event | category | flops | bytes accessed | tf_op | source)
XLA Modules:
  0.0 83.8 jit_solution(2762266087892091439)
XLA Ops:
  0.0 0.9 %maximum_bitcast_fusion = bf16[1,576,128]{2,1,0:T(8,128)(2,1)S(1)} fusion(bf16[64,128]{1,0:T(8,128)(2,1)} %param.14, bf16[512,128]{1,0:T(8,128)(2,1)} %param.13), kind=kLoop, calls=%fused_computation.1 | loop fusion | flops 294912 | bytes 294912 | tf_op jit(solution)/shard_map/broadcast_in_dim | solution.py:345
  0.9 0.1 collective-permute-start.3
  1.0 1.4 %collective-permute-done.3 = bf16[1,576,128]{2,1,0:T(8,128)(2,1)S(1)} collective-permute-done((bf16[1,576,128]{2,1,0:T(8,128)(2,1)S(1)}, bf16[1,576,128]{2,1,0:T(8,128)(2,1)S(1)}, u32[]{:S(2)}, u32[]{:S(2)}) %collective-permute-start.3) | collective-permute-done | bytes 147488 | tf_op jit(solution)/shard_map/ppermute | solution.py:72
  2.4 2.0 %collective-permute-start.4 = (bf16[2,576,128]{2,1,0:T(8,128)(2,1)S(1)}, bf16[2,576,128]{2,1,0:T(8,128)(2,1)S(1)}, u32[]{:S(2)}, u32[]{:S(2)}) collective-permute-start(bf16[2,576,128]{2,1,0:T(8,128)(2,1)S(1)} %pad_maximum_fusion), channel_id=1, source_target_pairs={{112,0},{97,1},{243,2},{226,3},{100,4},{117,5},{231,6},{246,7},{24... | collective-permute-start | bytes 884744 | tf_op jit(solution)/shard_map/ppermute | solution.py:72
  4.4 0.0 collective-permute-start.2
  5.7 6.8 %collective-permute-start.8 = (bf16[2,576,128]{2,1,0:T(8,128)(2,1)S(1)}, bf16[2,576,128]{2,1,0:T(8,128)(2,1)S(1)}, u32[]{:S(2)}, u32[]{:S(2)}) collective-permute-start(bf16[2,576,128]{2,1,0:T(8,128)(2,1)S(1)} %pad_maximum_fusion), channel_id=1, source_target_pairs={{80,0},{65,1},{211,2},{194,3},{68,4},{85,5},{199,6},{214,7},{56,8}... | collective-permute-start | bytes 884744 | tf_op jit(solution)/shard_map/ppermute | solution.py:72
  12.6 0.1 pad_add_fusion.refs_0_
  12.7 0.0 copy-start.1
  12.7 0.3 collective-permute-start
  12.9 0.0 collective-permute-done.4.refs_8_
  12.9 0.0 copy-start.5
  12.9 2.7 %collective-permute-start.5 = (bf16[2,576,128]{2,1,0:T(8,128)(2,1)S(1)}, bf16[2,576,128]{2,1,0:T(8,128)(2,1)S(1)}, u32[]{:S(2)}, u32[]{:S(2)}) collective-permute-start(bf16[2,576,128]{2,1,0:T(8,128)(2,1)S(1)} %collective-permute-done.4.refs_8_), channel_id=1, source_target_pairs={{6,0},{7,1},{0,2},{1,3},{2,4},{3,5},{4,6},{5,7},{14,8},{15,9},{8,1... | collective-permute-start | bytes 884744 | tf_op jit(solution)/shard_map/ppermute | solution.py:72
  15.6 2.8 %collective-permute-start.6 = (bf16[2,576,128]{2,1,0:T(8,128)(2,1)S(1)}, bf16[2,576,128]{2,1,0:T(8,128)(2,1)S(1)}, u32[]{:S(2)}, u32[]{:S(2)}) collective-permute-start(bf16[2,576,128]{2,1,0:T(8,128)(2,1)S(1)} %collective-permute-done.4.refs_8_), channel_id=1, source_target_pairs={{2,0},{3,1},{4,2},{5,3},{6,4},{7,5},{0,6},{1,7},{10,8},{11,9},{12,... | collective-permute-start | bytes 884744 | tf_op jit(solution)/shard_map/ppermute | solution.py:72
  18.5 0.0 collective-permute-done.refs_1_
  18.5 0.0 copy-start.3
  18.5 1.8 %collective-permute-start.7 = (bf16[2,576,128]{2,1,0:T(8,128)(2,1)S(1)}, bf16[2,576,128]{2,1,0:T(8,128)(2,1)S(1)}, u32[]{:S(2)}, u32[]{:S(2)}) collective-permute-start(bf16[2,576,128]{2,1,0:T(8,128)(2,1)S(1)} %collective-permute-done.4.refs_8_), channel_id=1, source_target_pairs={{1,0},{0,1},{3,2},{2,3},{5,4},{4,5},{7,6},{6,7},{9,8},{8,9},{11,10... | collective-permute-start | bytes 884744 | tf_op jit(solution)/shard_map/ppermute | solution.py:72
  20.3 0.0 collective-permute-done.2.refs_5_
  20.3 0.0 copy-start.10
  20.3 0.0 collective-permute-start.1
  20.3 2.8 %collective-permute-done.8.refs_4_ = bf16[2,576,128]{2,1,0:T(8,128)(2,1)S(1)} collective-permute-done((bf16[2,576,128]{2,1,0:T(8,128)(2,1)S(1)}, bf16[2,576,128]{2,1,0:T(8,128)(2,1)S(1)}, u32[]{:S(2)}, u32[]{:S(2)}) %collective-permute-start.8) | collective-permute-done | bytes 294944 | tf_op jit(solution)/shard_map/ppermute | solution.py:72
  23.1 3.3 %collective-permute-start.10 = (bf16[2,576,128]{2,1,0:T(8,128)(2,1)S(1)}, bf16[2,576,128]{2,1,0:T(8,128)(2,1)S(1)}, u32[]{:S(2)}, u32[]{:S(2)}) collective-permute-start(bf16[2,576,128]{2,1,0:T(8,128)(2,1)S(1)} %collective-permute-done.8.refs_4_), channel_id=1, source_target_pairs={{2,0},{3,1},{4,2},{5,3},{6,4},{7,5},{0,6},{1,7},{10,8},{11,9},{12,... | collective-permute-start | bytes 884744 | tf_op jit(solution)/shard_map/ppermute | solution.py:72
  26.4 0.0 collective-permute-done.1.refs_3_
  26.4 0.0 copy-start.9
  26.5 6.3 %collective-permute-start.11 = (bf16[2,576,128]{2,1,0:T(8,128)(2,1)S(1)}, bf16[2,576,128]{2,1,0:T(8,128)(2,1)S(1)}, u32[]{:S(2)}, u32[]{:S(2)}) collective-permute-start(bf16[2,576,128]{2,1,0:T(8,128)(2,1)S(1)} %collective-permute-done.8.refs_4_), channel_id=1, source_target_pairs={{1,0},{0,1},{3,2},{2,3},{5,4},{4,5},{7,6},{6,7},{9,8},{8,9},{11,10... | collective-permute-start | bytes 884744 | tf_op jit(solution)/shard_map/ppermute | solution.py:72
  32.7 0.0 collective-permute-done.5.refs_9_
  32.7 0.0 copy-start.6
  32.7 0.0 collective-permute-start.9
  32.8 0.0 collective-permute-done.6.refs_10_
  32.8 0.0 copy-start.7
  32.8 0.0 collective-permute-done.7.refs_11_
  32.8 0.0 copy-start.8
  32.8 0.0 copy-done.1
  32.8 0.0 copy-done.5
  32.8 0.0 copy-done.3
  32.8 0.0 copy-done.10
  32.8 0.0 copy-done.9
  32.8 0.6 copy-done.6
  33.5 0.1 copy-done.7
  33.6 0.1 copy-done.8
  33.7 13.8 %shard_map.109 = (bf16[1024,256]{1,0:T(8,128)(2,1)}, bf16[1024,256]{1,0:T(8,128)(2,1)}, bf16[2,1024,640]{2,1,0:T(8,128)(2,1)}) custom-call(s32[2]{0:T(128)} %copy-done.1, s32[2]{0:T(128)} %copy-done.3, bf16[1024,128]{1,0:T(8,128)(2,1)} %bitcast.12, bf16[1024,128]{1,0:T(8,128)(2,1)} %copy-done.9, bf16[8,64,128]{2,1,0:T(8,128)(2,1)} %bitcast.14, ...), custom_call_target="tpu_custom_call" | custom-call | flops 5435817984 | bytes 8388608 | tf_op jit(solution)/shard_map/pallas_call | solution.py:270
  47.5 0.0 collective-permute-done.10.refs_6_
  47.5 0.0 collective-permute-done.11.refs_7_
  47.5 0.0 collective-permute-done.9.refs_5_
  47.5 0.0 copy-start.2
  47.5 0.6 copy-done.2
  48.2 0.0 copy-start.4
  48.2 0.7 copy-done.4
  48.8 0.0 copy-start
  48.9 10.4 %shard_map.110 = (bf16[1024,256]{1,0:T(8,128)(2,1)S(1)}, bf16[1024,256]{1,0:T(8,128)(2,1)}) custom-call(s32[2]{0:T(128)S(1)} %copy-done.2, s32[2]{0:T(128)S(1)} %copy-done.4, bf16[2,1024,640]{2,1,0:T(8,128)(2,1)} %get-tuple-element.10.refs_2_, bf16[8,512,128]{2,1,0:T(8,128)(2,1)} %refs_3_.1, bf16[2,576,128]{2,1,0:T(8,128)(2,1)S(1)} %collective-permute-done.8.refs_4_, ...), custom_call_target="tpu_custom_call" | custom-call | flops 4831838208 | bytes 8388608 | tf_op jit(solution)/shard_map/pallas_call | solution.py:270
  59.2 0.1 collective-permute-start.12
  59.3 2.1 %collective-permute-done.12.refs_1_ = bf16[1024,256]{1,0:T(8,128)(2,1)S(1)} collective-permute-done((bf16[1024,256]{1,0:T(8,128)(2,1)}, bf16[1024,256]{1,0:T(8,128)(2,1)S(1)}, u32[]{:S(2)}, u32[]{:S(2)}) %collective-permute-start.12) | collective-permute-done | bytes 524320 | tf_op jit(solution)/shard_map/ppermute | solution.py:361
  61.4 0.0 copy-done
  61.4 2.9 %shard_map.111 = bf16[128,3584]{1,0:T(8,128)(2,1)S(1)} custom-call(s32[1]{0:T(128)S(6)} %copy.12.length_ref, bf16[1024,256]{1,0:T(8,128)(2,1)S(1)} %get-tuple-element.13.refs_0_, bf16[1024,256]{1,0:T(8,128)(2,1)S(1)} %collective-permute-done.12.refs_1_, bf16[1024,3584]{1,0:T(8,128)(2,1)S(1)} %bitcast.9), custom_call_target="tpu_custom_call" | custom-call | flops 939524096 | bytes 7340032 | tf_op jit(solution)/shard_map/pallas_call | solution.py:316
  64.4 18.7 %all_to_all.9 = bf16[8,16,3584]{2,1,0:T(8,128)(2,1)S(1)} all-to-all(bf16[8,16,3584]{2,1,0:T(8,128)(2,1)S(1)} %bitcast.10), channel_id=1, replica_groups=mesh['blk'=32,'head'=8] {'head'}, dimensions={0} | all-to-all | bytes 1835008 | tf_op jit(solution)/shard_map/all_to_all | solution.py:363
  83.0 0.8 reduce_sum.12
  (1 shorter events, 0.0 us)
Async XLA Ops:
  0.9 1.5 %collective-permute-start.3 = (bf16[1,576,128]{2,1,0:T(8,128)(2,1)S(1)}, bf16[1,576,128]{2,1,0:T(8,128)(2,1)S(1)}, u32[]{:S(2)}, u32[]{:S(2)}) collective-permute-start(bf16[1,576,128]{2,1,0:T(8,128)(2,1)S(1)} %maximum_bitcast_fusion), channel_id=1, source_target_pairs={{8,0},{9,1},{10,2},{11,3},{12,4},{13,5},{14,6},{15,7},{0,8},{1,9},... | collective-permute-start | bytes 442376 | tf_op jit(solution)/shard_map/ppermute | solution.py:72
  2.4 10.5 %collective-permute-start.4 = (bf16[2,576,128]{2,1,0:T(8,128)(2,1)S(1)}, bf16[2,576,128]{2,1,0:T(8,128)(2,1)S(1)}, u32[]{:S(2)}, u32[]{:S(2)}) collective-permute-start(bf16[2,576,128]{2,1,0:T(8,128)(2,1)S(1)} %pad_maximum_fusion), channel_id=1, source_target_pairs={{112,0},{97,1},{243,2},{226,3},{100,4},{117,5},{231,6},{246,7},{24... | collective-permute-start | bytes 884744 | tf_op jit(solution)/shard_map/ppermute | solution.py:72
  4.4 15.9 %collective-permute-start.2 = (bf16[8,64,128]{2,1,0:T(8,128)(2,1)}, bf16[8,64,128]{2,1,0:T(8,128)(2,1)S(1)}, u32[]{:S(2)}, u32[]{:S(2)}) collective-permute-start(bf16[8,64,128]{2,1,0:T(8,128)(2,1)} %bitcast.13), channel_id=1, source_target_pairs={{8,0},{9,1},{10,2},{11,3},{12,4},{13,5},{14,6},{15,7},{0,8},{1,9},... | collective-permute-start | bytes 393224 | tf_op jit(solution)/shard_map/ppermute | solution.py:356
  5.7 17.4 %collective-permute-start.8 = (bf16[2,576,128]{2,1,0:T(8,128)(2,1)S(1)}, bf16[2,576,128]{2,1,0:T(8,128)(2,1)S(1)}, u32[]{:S(2)}, u32[]{:S(2)}) collective-permute-start(bf16[2,576,128]{2,1,0:T(8,128)(2,1)S(1)} %pad_maximum_fusion), channel_id=1, source_target_pairs={{80,0},{65,1},{211,2},{194,3},{68,4},{85,5},{199,6},{214,7},{56,8}... | collective-permute-start | bytes 884744 | tf_op jit(solution)/shard_map/ppermute | solution.py:72
  12.7 20.1 %copy-start.1 = (s32[2]{0:T(128)}, s32[2]{0:T(128)S(1)}, u32[]{:S(2)}) copy-start(s32[2]{0:T(128)S(1)} %pad_add_fusion.refs_0_) | copy-start | bytes 28
  12.7 5.8 %collective-permute-start = (s32[2]{0:T(128)S(1)}, s32[2]{0:T(128)S(1)}, u32[]{:S(2)}, u32[]{:S(2)}) collective-permute-start(s32[2]{0:T(128)S(1)} %pad_add_fusion.refs_0_), channel_id=1, source_target_pairs={{8,0},{9,1},{10,2},{11,3},{12,4},{13,5},{14,6},{15,7},{0,8},{1,9},... | collective-permute-start | bytes 32 | tf_op jit(solution)/shard_map/ppermute | solution.py:353
  12.9 19.9 %copy-start.5 = (bf16[2,576,128]{2,1,0:T(8,128)(2,1)}, bf16[2,576,128]{2,1,0:T(8,128)(2,1)S(1)}, u32[]{:S(2)}) copy-start(bf16[2,576,128]{2,1,0:T(8,128)(2,1)S(1)} %collective-permute-done.4.refs_8_) | copy-start | bytes 884740
  12.9 19.8 %collective-permute-start.5 = (bf16[2,576,128]{2,1,0:T(8,128)(2,1)S(1)}, bf16[2,576,128]{2,1,0:T(8,128)(2,1)S(1)}, u32[]{:S(2)}, u32[]{:S(2)}) collective-permute-start(bf16[2,576,128]{2,1,0:T(8,128)(2,1)S(1)} %collective-permute-done.4.refs_8_), channel_id=1, source_target_pairs={{6,0},{7,1},{0,2},{1,3},{2,4},{3,5},{4,6},{5,7},{14,8},{15,9},{8,1... | collective-permute-start | bytes 884744 | tf_op jit(solution)/shard_map/ppermute | solution.py:72
  15.6 17.1 %collective-permute-start.6 = (bf16[2,576,128]{2,1,0:T(8,128)(2,1)S(1)}, bf16[2,576,128]{2,1,0:T(8,128)(2,1)S(1)}, u32[]{:S(2)}, u32[]{:S(2)}) collective-permute-start(bf16[2,576,128]{2,1,0:T(8,128)(2,1)S(1)} %collective-permute-done.4.refs_8_), channel_id=1, source_target_pairs={{2,0},{3,1},{4,2},{5,3},{6,4},{7,5},{0,6},{1,7},{10,8},{11,9},{12,... | collective-permute-start | bytes 884744 | tf_op jit(solution)/shard_map/ppermute | solution.py:72
  18.5 14.3 %copy-start.3 = (s32[2]{0:T(128)}, s32[2]{0:T(128)S(1)}, u32[]{:S(2)}) copy-start(s32[2]{0:T(128)S(1)} %collective-permute-done.refs_1_) | copy-start | bytes 28
  18.5 14.3 %collective-permute-start.7 = (bf16[2,576,128]{2,1,0:T(8,128)(2,1)S(1)}, bf16[2,576,128]{2,1,0:T(8,128)(2,1)S(1)}, u32[]{:S(2)}, u32[]{:S(2)}) collective-permute-start(bf16[2,576,128]{2,1,0:T(8,128)(2,1)S(1)} %collective-permute-done.4.refs_8_), channel_id=1, source_target_pairs={{1,0},{0,1},{3,2},{2,3},{5,4},{4,5},{7,6},{6,7},{9,8},{8,9},{11,10... | collective-permute-start | bytes 884744 | tf_op jit(solution)/shard_map/ppermute | solution.py:72
  20.3 12.5 %copy-start.10 = (bf16[8,64,128]{2,1,0:T(8,128)(2,1)}, bf16[8,64,128]{2,1,0:T(8,128)(2,1)S(1)}, u32[]{:S(2)}) copy-start(bf16[8,64,128]{2,1,0:T(8,128)(2,1)S(1)} %collective-permute-done.2.refs_5_) | copy-start | bytes 393220
  20.3 6.1 %collective-permute-start.1 = (bf16[1024,128]{1,0:T(8,128)(2,1)}, bf16[1024,128]{1,0:T(8,128)(2,1)S(1)}, u32[]{:S(2)}, u32[]{:S(2)}) collective-permute-start(bf16[1024,128]{1,0:T(8,128)(2,1)} %bitcast.11), channel_id=1, source_target_pairs={{8,0},{9,1},{10,2},{11,3},{12,4},{13,5},{14,6},{15,7},{0,8},{1,9},... | collective-permute-start | bytes 786440 | tf_op jit(solution)/shard_map/ppermute | solution.py:356
  23.1 24.3 %collective-permute-start.10 = (bf16[2,576,128]{2,1,0:T(8,128)(2,1)S(1)}, bf16[2,576,128]{2,1,0:T(8,128)(2,1)S(1)}, u32[]{:S(2)}, u32[]{:S(2)}) collective-permute-start(bf16[2,576,128]{2,1,0:T(8,128)(2,1)S(1)} %collective-permute-done.8.refs_4_), channel_id=1, source_target_pairs={{2,0},{3,1},{4,2},{5,3},{6,4},{7,5},{0,6},{1,7},{10,8},{11,9},{12,... | collective-permute-start | bytes 884744 | tf_op jit(solution)/shard_map/ppermute | solution.py:72
  26.4 6.4 %copy-start.9 = (bf16[1024,128]{1,0:T(8,128)(2,1)}, bf16[1024,128]{1,0:T(8,128)(2,1)S(1)}, u32[]{:S(2)}) copy-start(bf16[1024,128]{1,0:T(8,128)(2,1)S(1)} %collective-permute-done.1.refs_3_) | copy-start | bytes 786436
  26.5 21.0 %collective-permute-start.11 = (bf16[2,576,128]{2,1,0:T(8,128)(2,1)S(1)}, bf16[2,576,128]{2,1,0:T(8,128)(2,1)S(1)}, u32[]{:S(2)}, u32[]{:S(2)}) collective-permute-start(bf16[2,576,128]{2,1,0:T(8,128)(2,1)S(1)} %collective-permute-done.8.refs_4_), channel_id=1, source_target_pairs={{1,0},{0,1},{3,2},{2,3},{5,4},{4,5},{7,6},{6,7},{9,8},{8,9},{11,10... | collective-permute-start | bytes 884744 | tf_op jit(solution)/shard_map/ppermute | solution.py:72
  32.7 0.7 copy-start.6
  32.7 14.8 %collective-permute-start.9 = (bf16[2,576,128]{2,1,0:T(8,128)(2,1)S(1)}, bf16[2,576,128]{2,1,0:T(8,128)(2,1)S(1)}, u32[]{:S(2)}, u32[]{:S(2)}) collective-permute-start(bf16[2,576,128]{2,1,0:T(8,128)(2,1)S(1)} %collective-permute-done.8.refs_4_), channel_id=1, source_target_pairs={{6,0},{7,1},{0,2},{1,3},{2,4},{3,5},{4,6},{5,7},{14,8},{15,9},{8,1... | collective-permute-start | bytes 884744 | tf_op jit(solution)/shard_map/ppermute | solution.py:72
  32.8 0.8 copy-start.7
  32.8 0.9 %copy-start.8 = (bf16[2,576,128]{2,1,0:T(8,128)(2,1)}, bf16[2,576,128]{2,1,0:T(8,128)(2,1)S(1)}, u32[]{:S(2)}) copy-start(bf16[2,576,128]{2,1,0:T(8,128)(2,1)S(1)} %collective-permute-done.7.refs_11_) | copy-start | bytes 884740
  47.5 0.7 copy-start.2
  48.2 0.7 copy-start.4
  48.8 12.6 %copy-start = (bf16[8,128,3584]{2,1,0:T(8,128)(2,1)S(1)}, bf16[8,128,3584]{2,1,0:T(8,128)(2,1)}, u32[]{:S(2)}) copy-start(bf16[8,128,3584]{2,1,0:T(8,128)(2,1)} %param.19) | copy-start | bytes 22020100
  59.2 2.2 %collective-permute-start.12 = (bf16[1024,256]{1,0:T(8,128)(2,1)}, bf16[1024,256]{1,0:T(8,128)(2,1)S(1)}, u32[]{:S(2)}, u32[]{:S(2)}) collective-permute-start(bf16[1024,256]{1,0:T(8,128)(2,1)} %get-tuple-element.14), channel_id=1, source_target_pairs={{8,0},{9,1},{10,2},{11,3},{12,4},{13,5},{14,6},{15,7},{0,8},{1,9},... | collective-permute-start | bytes 1572872 | tf_op jit(solution)/shard_map/ppermute | solution.py:361

commit v4 on v3

--- a/solution.py
+++ b/solution.py
@@ -297,33 +297,29 @@
     def kernel(length_ref, *refs):
         piece_refs = refs[: len(pieces)]
         weight_ref, out_ref, values = refs[len(pieces) :]
-
-        @pl.when(pl.program_id(0) == 0)
-        def _():
-            for head in range(heads):
-                part = slice(head * KEYS, (head + 1) * KEYS)
-                levels = [level_of(ref[part, KEYS:]) for ref in piece_refs]
-                top = functools.reduce(jnp.maximum, levels)
-                shares = [jnp.exp2(level - top) for level in levels]
-                both = functools.reduce(
-                    jnp.add, [ref[part, :KEYS].astype(jnp.float32) * s for ref, s in zip(piece_refs, shares)]
-                ) / functools.reduce(jnp.add, shares)
-                slot = lax.broadcasted_iota(jnp.int32, (KEYS, KEYS), 0)
-                values[:, part] = jnp.where(slot < length_ref[0], both, 0.0).astype(jnp.bfloat16)
-
-        out_ref[...] = jnp.dot(values[...], weight_ref[...], preferred_element_type=jnp.float32).astype(jnp.bfloat16)
-
+        for head in range(heads):
+            part = slice(head * KEYS, (head + 1) * KEYS)
+            levels = [level_of(ref[part, KEYS:]) for ref in piece_refs]
+            top = functools.reduce(jnp.maximum, levels)
+            shares = [jnp.exp2(level - top) for level in levels]
+            both = functools.reduce(
+                jnp.add, [ref[part, :KEYS].astype(jnp.float32) * s for ref, s in zip(piece_refs, shares)]
+            ) / functools.reduce(jnp.add, shares)
+            slot = lax.broadcasted_iota(jnp.int32, (KEYS, KEYS), 0)
+            values[:, part] = jnp.where(slot < length_ref[0], both, 0.0).astype(jnp.bfloat16)
+
+        for begin in range(0, width, tile):
+            part = slice(begin, begin + tile)
+            found = jnp.dot(values[...], weight_ref[:, part], preferred_element_type=jnp.float32)
+            out_ref[:, part] = found.astype(jnp.bfloat16)
+
+    vmem = pl.BlockSpec(memory_space=pltpu.VMEM)
     return pl.pallas_call(
         kernel,
-        grid_spec=pltpu.PrefetchScalarGridSpec(
-            num_scalar_prefetch=1,
-            grid=(width // tile,),
-            in_specs=[pl.BlockSpec(p.shape, lambda i, *_: (0, 0)) for p in pieces]
-            + [pl.BlockSpec((rows, tile), lambda i, *_: (0, i))],
-            out_specs=pl.BlockSpec((KEYS, tile), lambda i, *_: (0, i)),
-            scratch_shapes=[pltpu.VMEM((KEYS, rows), jnp.bfloat16)],
-        ),
+        in_specs=[pl.BlockSpec(memory_space=pltpu.SMEM)] + [vmem] * (len(pieces) + 1),
+        out_specs=vmem,
         out_shape=jax.ShapeDtypeStruct((KEYS, width), jnp.bfloat16),
+        scratch_shapes=[pltpu.VMEM((KEYS, rows), jnp.bfloat16)],
         compiler_params=pltpu.CompilerParams(vmem_limit_bytes=24 * 2**20),
         cost_estimate=pl.CostEstimate(flops=2 * KEYS * rows * width, bytes_accessed=2 * rows * width, transcendentals=0),
     )(length, *pieces, output_weight)

time: 83.3 us -> 82.3 us (0.988); the launches traced: 83.8 us -> 80.9 us
  Pallas kernels: 27.1 us -> 24.2 us
    pallas_call x2, Pallas kernels: 24.2 us -> 22.7 us  [attend(): pl.pallas_call(kernel, in_specs=[smem] * 2 + [hbm] * (len(operands) - 2),...]
    pallas_call x1, Pallas kernels: 2.93 us -> 1.53 us  [project(): pl.pallas_call(kernel, in_specs=[pl.BlockSpec(memory_space=pltpu.SMEM)] +...]
  transfers between devices with their start and end apart: 13 -> 13, of which waited for: 3 -> 3; matrix products, arithmetic and copies ran while one was open for 0% -> 0% of each run, Pallas kernels for 16% -> 15%
where the time goes in v4:
time: 82.3 us; the launch traced here: 80.9 us
  starting transfers between devices  26.2 us (32%)
  Pallas kernels  24.2 us (29%)
  blocking collectives  18.7 us (23%)
  waiting for transfers between devices  6.33 us (8%)
  local copies, waits for them, and re-layouts  2.18 us (3%)
  other arithmetic  1.82 us (2%)
  between operations  1.48 us (2%)
    ppermute x9, starting transfers between devices, taken(): lax.ppermute(self.array, AXES, pairs_from(source))  25.9 us
    pallas_call x2, Pallas kernels, attend(): pl.pallas_call(kernel, in_specs=[smem] * 2 + [hbm] * (len(operands) - 2),...  22.7 us
    all_to_all x1, blocking collectives, body(): parts = lax.all_to_all(term, 'head', 0, 0, tiled=True)  18.7 us
    ppermute x9, waiting for transfers between devices, taken(): lax.ppermute(self.array, AXES, pairs_from(source))  4.22 us
    unnamed x22, local copies, waits for them, and re-layouts  2.18 us
    ppermute x1, waiting for transfers between devices, body(): pieces = (mine_part, lax.ppermute(sent, AXES, partner))  2.11 us
  transfers between devices with their start and end apart: 13, of which 3 were waited for; matrix products, arithmetic and copies ran while one was open for 0% of the time, Pallas kernels for 15%

profile of v4, /device:TPU:48, one launch (start us, length us, event | category | flops | bytes accessed | tf_op | source)
XLA Modules:
  0.0 80.9 jit_solution(2402634143077924602)
XLA Ops:
  0.0 0.9 %maximum_bitcast_fusion = bf16[1,576,128]{2,1,0:T(8,128)(2,1)S(1)} fusion(bf16[64,128]{1,0:T(8,128)(2,1)} %param.14, bf16[512,128]{1,0:T(8,128)(2,1)} %param.13), kind=kLoop, calls=%fused_computation.1 | loop fusion | flops 294912 | bytes 294912 | tf_op jit(solution)/shard_map/broadcast_in_dim | solution.py:341
  0.9 0.1 collective-permute-start.3
  1.0 1.4 %collective-permute-done.3 = bf16[1,576,128]{2,1,0:T(8,128)(2,1)S(1)} collective-permute-done((bf16[1,576,128]{2,1,0:T(8,128)(2,1)S(1)}, bf16[1,576,128]{2,1,0:T(8,128)(2,1)S(1)}, u32[]{:S(2)}, u32[]{:S(2)}) %collective-permute-start.3) | collective-permute-done | bytes 147488 | tf_op jit(solution)/shard_map/ppermute | solution.py:72
  2.4 2.0 %collective-permute-start.4 = (bf16[2,576,128]{2,1,0:T(8,128)(2,1)S(1)}, bf16[2,576,128]{2,1,0:T(8,128)(2,1)S(1)}, u32[]{:S(2)}, u32[]{:S(2)}) collective-permute-start(bf16[2,576,128]{2,1,0:T(8,128)(2,1)S(1)} %pad_maximum_fusion), channel_id=1, source_target_pairs={{112,0},{97,1},{243,2},{226,3},{100,4},{117,5},{231,6},{246,7},{24... | collective-permute-start | bytes 884744 | tf_op jit(solution)/shard_map/ppermute | solution.py:72
  4.4 0.0 collective-permute-start.2
  5.7 6.8 %collective-permute-start.8 = (bf16[2,576,128]{2,1,0:T(8,128)(2,1)S(1)}, bf16[2,576,128]{2,1,0:T(8,128)(2,1)S(1)}, u32[]{:S(2)}, u32[]{:S(2)}) collective-permute-start(bf16[2,576,128]{2,1,0:T(8,128)(2,1)S(1)} %pad_maximum_fusion), channel_id=1, source_target_pairs={{80,0},{65,1},{211,2},{194,3},{68,4},{85,5},{199,6},{214,7},{56,8}... | collective-permute-start | bytes 884744 | tf_op jit(solution)/shard_map/ppermute | solution.py:72
  12.6 0.1 pad_add_fusion.refs_0_
  12.7 0.0 copy-start.1
  12.7 0.3 collective-permute-start
  12.9 0.0 collective-permute-done.4.refs_8_
  12.9 0.0 copy-start.5
  12.9 2.7 %collective-permute-start.5 = (bf16[2,576,128]{2,1,0:T(8,128)(2,1)S(1)}, bf16[2,576,128]{2,1,0:T(8,128)(2,1)S(1)}, u32[]{:S(2)}, u32[]{:S(2)}) collective-permute-start(bf16[2,576,128]{2,1,0:T(8,128)(2,1)S(1)} %collective-permute-done.4.refs_8_), channel_id=1, source_target_pairs={{6,0},{7,1},{0,2},{1,3},{2,4},{3,5},{4,6},{5,7},{14,8},{15,9},{8,1... | collective-permute-start | bytes 884744 | tf_op jit(solution)/shard_map/ppermute | solution.py:72
  15.6 2.8 %collective-permute-start.6 = (bf16[2,576,128]{2,1,0:T(8,128)(2,1)S(1)}, bf16[2,576,128]{2,1,0:T(8,128)(2,1)S(1)}, u32[]{:S(2)}, u32[]{:S(2)}) collective-permute-start(bf16[2,576,128]{2,1,0:T(8,128)(2,1)S(1)} %collective-permute-done.4.refs_8_), channel_id=1, source_target_pairs={{2,0},{3,1},{4,2},{5,3},{6,4},{7,5},{0,6},{1,7},{10,8},{11,9},{12,... | collective-permute-start | bytes 884744 | tf_op jit(solution)/shard_map/ppermute | solution.py:72
  18.5 0.0 collective-permute-done.refs_1_
  18.5 0.0 copy-start.3
  18.5 1.8 %collective-permute-start.7 = (bf16[2,576,128]{2,1,0:T(8,128)(2,1)S(1)}, bf16[2,576,128]{2,1,0:T(8,128)(2,1)S(1)}, u32[]{:S(2)}, u32[]{:S(2)}) collective-permute-start(bf16[2,576,128]{2,1,0:T(8,128)(2,1)S(1)} %collective-permute-done.4.refs_8_), channel_id=1, source_target_pairs={{1,0},{0,1},{3,2},{2,3},{5,4},{4,5},{7,6},{6,7},{9,8},{8,9},{11,10... | collective-permute-start | bytes 884744 | tf_op jit(solution)/shard_map/ppermute | solution.py:72
  20.3 0.0 collective-permute-done.2.refs_5_
  20.3 0.0 copy-start.10
  20.3 0.0 collective-permute-start.1
  20.3 2.8 %collective-permute-done.8.refs_4_ = bf16[2,576,128]{2,1,0:T(8,128)(2,1)S(1)} collective-permute-done((bf16[2,576,128]{2,1,0:T(8,128)(2,1)S(1)}, bf16[2,576,128]{2,1,0:T(8,128)(2,1)S(1)}, u32[]{:S(2)}, u32[]{:S(2)}) %collective-permute-start.8) | collective-permute-done | bytes 294944 | tf_op jit(solution)/shard_map/ppermute | solution.py:72
  23.1 3.3 %collective-permute-start.10 = (bf16[2,576,128]{2,1,0:T(8,128)(2,1)S(1)}, bf16[2,576,128]{2,1,0:T(8,128)(2,1)S(1)}, u32[]{:S(2)}, u32[]{:S(2)}) collective-permute-start(bf16[2,576,128]{2,1,0:T(8,128)(2,1)S(1)} %collective-permute-done.8.refs_4_), channel_id=1, source_target_pairs={{2,0},{3,1},{4,2},{5,3},{6,4},{7,5},{0,6},{1,7},{10,8},{11,9},{12,... | collective-permute-start | bytes 884744 | tf_op jit(solution)/shard_map/ppermute | solution.py:72
  26.4 0.0 collective-permute-done.1.refs_3_
  26.4 0.0 copy-start.9
  26.5 6.3 %collective-permute-start.11 = (bf16[2,576,128]{2,1,0:T(8,128)(2,1)S(1)}, bf16[2,576,128]{2,1,0:T(8,128)(2,1)S(1)}, u32[]{:S(2)}, u32[]{:S(2)}) collective-permute-start(bf16[2,576,128]{2,1,0:T(8,128)(2,1)S(1)} %collective-permute-done.8.refs_4_), channel_id=1, source_target_pairs={{1,0},{0,1},{3,2},{2,3},{5,4},{4,5},{7,6},{6,7},{9,8},{8,9},{11,10... | collective-permute-start | bytes 884744 | tf_op jit(solution)/shard_map/ppermute | solution.py:72
  32.7 0.0 collective-permute-done.5.refs_9_
  32.7 0.0 copy-start.6
  32.7 0.0 collective-permute-start.9
  32.8 0.0 collective-permute-done.6.refs_10_
  32.8 0.0 copy-start.7
  32.8 0.0 collective-permute-done.7.refs_11_
  32.8 0.0 copy-start.8
  32.8 0.0 copy-done.1
  32.8 0.0 copy-done.5
  32.8 0.0 copy-done.3
  32.8 0.0 copy-done.10
  32.8 0.0 copy-done.9
  32.8 0.6 copy-done.6
  33.5 0.1 copy-done.7
  33.6 0.1 copy-done.8
  33.7 12.3 %shard_map.109 = (bf16[1024,256]{1,0:T(8,128)(2,1)}, bf16[1024,256]{1,0:T(8,128)(2,1)}, bf16[2,1024,640]{2,1,0:T(8,128)(2,1)}) custom-call(s32[2]{0:T(128)} %copy-done.1, s32[2]{0:T(128)} %copy-done.3, bf16[1024,128]{1,0:T(8,128)(2,1)} %bitcast.12, bf16[1024,128]{1,0:T(8,128)(2,1)} %copy-done.9, bf16[8,64,128]{2,1,0:T(8,128)(2,1)} %bitcast.14, ...), custom_call_target="tpu_custom_call" | custom-call | flops 5435817984 | bytes 8388608 | tf_op jit(solution)/shard_map/pallas_call | solution.py:270
  46.0 0.0 collective-permute-done.10.refs_6_
  46.0 0.0 collective-permute-done.11.refs_7_
  46.0 0.0 collective-permute-done.9.refs_5_
  46.0 0.0 copy-start.2
  46.0 0.6 copy-done.2
  46.7 0.0 copy-start.4
  46.7 0.7 copy-done.4
  47.4 0.0 copy-start
  47.4 10.4 %shard_map.110 = (bf16[1024,256]{1,0:T(8,128)(2,1)S(1)}, bf16[1024,256]{1,0:T(8,128)(2,1)}) custom-call(s32[2]{0:T(128)S(1)} %copy-done.2, s32[2]{0:T(128)S(1)} %copy-done.4, bf16[2,1024,640]{2,1,0:T(8,128)(2,1)} %get-tuple-element.10.refs_2_, bf16[8,512,128]{2,1,0:T(8,128)(2,1)} %refs_3_.1, bf16[2,576,128]{2,1,0:T(8,128)(2,1)S(1)} %collective-permute-done.8.refs_4_, ...), custom_call_target="tpu_custom_call" | custom-call | flops 4831838208 | bytes 8388608 | tf_op jit(solution)/shard_map/pallas_call | solution.py:270
  57.7 0.1 collective-permute-start.12
  57.8 2.1 %collective-permute-done.12.refs_1_ = bf16[1024,256]{1,0:T(8,128)(2,1)S(1)} collective-permute-done((bf16[1024,256]{1,0:T(8,128)(2,1)}, bf16[1024,256]{1,0:T(8,128)(2,1)S(1)}, u32[]{:S(2)}, u32[]{:S(2)}) %collective-permute-start.12) | collective-permute-done | bytes 524320 | tf_op jit(solution)/shard_map/ppermute | solution.py:357
  59.9 0.0 copy-done
  59.9 1.5 %shard_map.111 = bf16[128,3584]{1,0:T(8,128)(2,1)S(1)} custom-call(s32[1]{0:T(128)S(6)} %copy.12.length_ref, bf16[1024,256]{1,0:T(8,128)(2,1)S(1)} %get-tuple-element.13.refs_0_, bf16[1024,256]{1,0:T(8,128)(2,1)S(1)} %collective-permute-done.12.refs_1_, bf16[1024,3584]{1,0:T(8,128)(2,1)S(1)} %bitcast.9), custom_call_target="tpu_custom_call" | custom-call | flops 939524096 | bytes 7340032 | tf_op jit(solution)/shard_map/pallas_call | solution.py:317
  61.5 18.7 %all_to_all.9 = bf16[8,16,3584]{2,1,0:T(8,128)(2,1)S(1)} all-to-all(bf16[8,16,3584]{2,1,0:T(8,128)(2,1)S(1)} %bitcast.10), channel_id=1, replica_groups=mesh['blk'=32,'head'=8] {'head'}, dimensions={0} | all-to-all | bytes 1835008 | tf_op jit(solution)/shard_map/all_to_all | solution.py:359
  80.1 0.8 reduce_sum.12
  (1 shorter events, 0.0 us)
Async XLA Ops:
  0.9 1.5 %collective-permute-start.3 = (bf16[1,576,128]{2,1,0:T(8,128)(2,1)S(1)}, bf16[1,576,128]{2,1,0:T(8,128)(2,1)S(1)}, u32[]{:S(2)}, u32[]{:S(2)}) collective-permute-start(bf16[1,576,128]{2,1,0:T(8,128)(2,1)S(1)} %maximum_bitcast_fusion), channel_id=1, source_target_pairs={{8,0},{9,1},{10,2},{11,3},{12,4},{13,5},{14,6},{15,7},{0,8},{1,9},... | collective-permute-start | bytes 442376 | tf_op jit(solution)/shard_map/ppermute | solution.py:72
  2.4 10.5 %collective-permute-start.4 = (bf16[2,576,128]{2,1,0:T(8,128)(2,1)S(1)}, bf16[2,576,128]{2,1,0:T(8,128)(2,1)S(1)}, u32[]{:S(2)}, u32[]{:S(2)}) collective-permute-start(bf16[2,576,128]{2,1,0:T(8,128)(2,1)S(1)} %pad_maximum_fusion), channel_id=1, source_target_pairs={{112,0},{97,1},{243,2},{226,3},{100,4},{117,5},{231,6},{246,7},{24... | collective-permute-start | bytes 884744 | tf_op jit(solution)/shard_map/ppermute | solution.py:72
  4.4 15.9 %collective-permute-start.2 = (bf16[8,64,128]{2,1,0:T(8,128)(2,1)}, bf16[8,64,128]{2,1,0:T(8,128)(2,1)S(1)}, u32[]{:S(2)}, u32[]{:S(2)}) collective-permute-start(bf16[8,64,128]{2,1,0:T(8,128)(2,1)} %bitcast.13), channel_id=1, source_target_pairs={{8,0},{9,1},{10,2},{11,3},{12,4},{13,5},{14,6},{15,7},{0,8},{1,9},... | collective-permute-start | bytes 393224 | tf_op jit(solution)/shard_map/ppermute | solution.py:352
  5.7 17.4 %collective-permute-start.8 = (bf16[2,576,128]{2,1,0:T(8,128)(2,1)S(1)}, bf16[2,576,128]{2,1,0:T(8,128)(2,1)S(1)}, u32[]{:S(2)}, u32[]{:S(2)}) collective-permute-start(bf16[2,576,128]{2,1,0:T(8,128)(2,1)S(1)} %pad_maximum_fusion), channel_id=1, source_target_pairs={{80,0},{65,1},{211,2},{194,3},{68,4},{85,5},{199,6},{214,7},{56,8}... | collective-permute-start | bytes 884744 | tf_op jit(solution)/shard_map/ppermute | solution.py:72
  12.7 20.1 %copy-start.1 = (s32[2]{0:T(128)}, s32[2]{0:T(128)S(1)}, u32[]{:S(2)}) copy-start(s32[2]{0:T(128)S(1)} %pad_add_fusion.refs_0_) | copy-start | bytes 28
  12.7 5.8 %collective-permute-start = (s32[2]{0:T(128)S(1)}, s32[2]{0:T(128)S(1)}, u32[]{:S(2)}, u32[]{:S(2)}) collective-permute-start(s32[2]{0:T(128)S(1)} %pad_add_fusion.refs_0_), channel_id=1, source_target_pairs={{8,0},{9,1},{10,2},{11,3},{12,4},{13,5},{14,6},{15,7},{0,8},{1,9},... | collective-permute-start | bytes 32 | tf_op jit(solution)/shard_map/ppermute | solution.py:349
  12.9 19.9 %copy-start.5 = (bf16[2,576,128]{2,1,0:T(8,128)(2,1)}, bf16[2,576,128]{2,1,0:T(8,128)(2,1)S(1)}, u32[]{:S(2)}) copy-start(bf16[2,576,128]{2,1,0:T(8,128)(2,1)S(1)} %collective-permute-done.4.refs_8_) | copy-start | bytes 884740
  12.9 19.8 %collective-permute-start.5 = (bf16[2,576,128]{2,1,0:T(8,128)(2,1)S(1)}, bf16[2,576,128]{2,1,0:T(8,128)(2,1)S(1)}, u32[]{:S(2)}, u32[]{:S(2)}) collective-permute-start(bf16[2,576,128]{2,1,0:T(8,128)(2,1)S(1)} %collective-permute-done.4.refs_8_), channel_id=1, source_target_pairs={{6,0},{7,1},{0,2},{1,3},{2,4},{3,5},{4,6},{5,7},{14,8},{15,9},{8,1... | collective-permute-start | bytes 884744 | tf_op jit(solution)/shard_map/ppermute | solution.py:72
  15.6 17.1 %collective-permute-start.6 = (bf16[2,576,128]{2,1,0:T(8,128)(2,1)S(1)}, bf16[2,576,128]{2,1,0:T(8,128)(2,1)S(1)}, u32[]{:S(2)}, u32[]{:S(2)}) collective-permute-start(bf16[2,576,128]{2,1,0:T(8,128)(2,1)S(1)} %collective-permute-done.4.refs_8_), channel_id=1, source_target_pairs={{2,0},{3,1},{4,2},{5,3},{6,4},{7,5},{0,6},{1,7},{10,8},{11,9},{12,... | collective-permute-start | bytes 884744 | tf_op jit(solution)/shard_map/ppermute | solution.py:72
  18.5 14.3 %copy-start.3 = (s32[2]{0:T(128)}, s32[2]{0:T(128)S(1)}, u32[]{:S(2)}) copy-start(s32[2]{0:T(128)S(1)} %collective-permute-done.refs_1_) | copy-start | bytes 28
  18.5 14.3 %collective-permute-start.7 = (bf16[2,576,128]{2,1,0:T(8,128)(2,1)S(1)}, bf16[2,576,128]{2,1,0:T(8,128)(2,1)S(1)}, u32[]{:S(2)}, u32[]{:S(2)}) collective-permute-start(bf16[2,576,128]{2,1,0:T(8,128)(2,1)S(1)} %collective-permute-done.4.refs_8_), channel_id=1, source_target_pairs={{1,0},{0,1},{3,2},{2,3},{5,4},{4,5},{7,6},{6,7},{9,8},{8,9},{11,10... | collective-permute-start | bytes 884744 | tf_op jit(solution)/shard_map/ppermute | solution.py:72
  20.3 12.5 %copy-start.10 = (bf16[8,64,128]{2,1,0:T(8,128)(2,1)}, bf16[8,64,128]{2,1,0:T(8,128)(2,1)S(1)}, u32[]{:S(2)}) copy-start(bf16[8,64,128]{2,1,0:T(8,128)(2,1)S(1)} %collective-permute-done.2.refs_5_) | copy-start | bytes 393220
  20.3 6.1 %collective-permute-start.1 = (bf16[1024,128]{1,0:T(8,128)(2,1)}, bf16[1024,128]{1,0:T(8,128)(2,1)S(1)}, u32[]{:S(2)}, u32[]{:S(2)}) collective-permute-start(bf16[1024,128]{1,0:T(8,128)(2,1)} %bitcast.11), channel_id=1, source_target_pairs={{8,0},{9,1},{10,2},{11,3},{12,4},{13,5},{14,6},{15,7},{0,8},{1,9},... | collective-permute-start | bytes 786440 | tf_op jit(solution)/shard_map/ppermute | solution.py:352
  23.1 22.9 %collective-permute-start.10 = (bf16[2,576,128]{2,1,0:T(8,128)(2,1)S(1)}, bf16[2,576,128]{2,1,0:T(8,128)(2,1)S(1)}, u32[]{:S(2)}, u32[]{:S(2)}) collective-permute-start(bf16[2,576,128]{2,1,0:T(8,128)(2,1)S(1)} %collective-permute-done.8.refs_4_), channel_id=1, source_target_pairs={{2,0},{3,1},{4,2},{5,3},{6,4},{7,5},{0,6},{1,7},{10,8},{11,9},{12,... | collective-permute-start | bytes 884744 | tf_op jit(solution)/shard_map/ppermute | solution.py:72
  26.4 6.4 %copy-start.9 = (bf16[1024,128]{1,0:T(8,128)(2,1)}, bf16[1024,128]{1,0:T(8,128)(2,1)S(1)}, u32[]{:S(2)}) copy-start(bf16[1024,128]{1,0:T(8,128)(2,1)S(1)} %collective-permute-done.1.refs_3_) | copy-start | bytes 786436
  26.5 19.6 %collective-permute-start.11 = (bf16[2,576,128]{2,1,0:T(8,128)(2,1)S(1)}, bf16[2,576,128]{2,1,0:T(8,128)(2,1)S(1)}, u32[]{:S(2)}, u32[]{:S(2)}) collective-permute-start(bf16[2,576,128]{2,1,0:T(8,128)(2,1)S(1)} %collective-permute-done.8.refs_4_), channel_id=1, source_target_pairs={{1,0},{0,1},{3,2},{2,3},{5,4},{4,5},{7,6},{6,7},{9,8},{8,9},{11,10... | collective-permute-start | bytes 884744 | tf_op jit(solution)/shard_map/ppermute | solution.py:72
  32.7 0.7 copy-start.6
  32.7 13.3 %collective-permute-start.9 = (bf16[2,576,128]{2,1,0:T(8,128)(2,1)S(1)}, bf16[2,576,128]{2,1,0:T(8,128)(2,1)S(1)}, u32[]{:S(2)}, u32[]{:S(2)}) collective-permute-start(bf16[2,576,128]{2,1,0:T(8,128)(2,1)S(1)} %collective-permute-done.8.refs_4_), channel_id=1, source_target_pairs={{6,0},{7,1},{0,2},{1,3},{2,4},{3,5},{4,6},{5,7},{14,8},{15,9},{8,1... | collective-permute-start | bytes 884744 | tf_op jit(solution)/shard_map/ppermute | solution.py:72
  32.8 0.8 copy-start.7
  32.8 0.9 %copy-start.8 = (bf16[2,576,128]{2,1,0:T(8,128)(2,1)}, bf16[2,576,128]{2,1,0:T(8,128)(2,1)S(1)}, u32[]{:S(2)}) copy-start(bf16[2,576,128]{2,1,0:T(8,128)(2,1)S(1)} %collective-permute-done.7.refs_11_) | copy-start | bytes 884740
  46.0 0.7 copy-start.2
  46.7 0.7 copy-start.4
  47.4 12.6 %copy-start = (bf16[8,128,3584]{2,1,0:T(8,128)(2,1)S(1)}, bf16[8,128,3584]{2,1,0:T(8,128)(2,1)}, u32[]{:S(2)}) copy-start(bf16[8,128,3584]{2,1,0:T(8,128)(2,1)} %param.19) | copy-start | bytes 22020100
  57.7 2.2 %collective-permute-start.12 = (bf16[1024,256]{1,0:T(8,128)(2,1)}, bf16[1024,256]{1,0:T(8,128)(2,1)S(1)}, u32[]{:S(2)}, u32[]{:S(2)}) collective-permute-start(bf16[1024,256]{1,0:T(8,128)(2,1)} %get-tuple-element.14), channel_id=1, source_target_pairs={{8,0},{9,1},{10,2},{11,3},{12,4},{13,5},{14,6},{15,7},{0,8},{1,9},... | collective-permute-start | bytes 1572872 | tf_op jit(solution)/shard_map/ppermute | solution.py:357
